TPU v7x, 32 devices: a whole 2x2x4 slice. The times are simulated.
32 devices in a mesh: ctx: 4 (over z), exp: 8 (over y, x, core).
Axes of the slice: x: 2, y: 2, z: 4, core: 2. Of those that a mesh axis runs over, the one named last changes fastest.
Arguments:
- tokens: bfloat16 [4096, 2048], P(('ctx', 'exp')), may hold values from -6 to 6
- expert_ids: int32 [4096, 1], P(('ctx', 'exp')), may hold values from 0 to 7; in each aligned block of 128 rows (0 to 127, 128 to 255, ...) at most 20 rows name the same one
- gate_weights: float32 [4096, 1], P(('ctx', 'exp')), may hold values from 0.1 to 1
- weight_gate: bfloat16 [8, 2048, 1024], P('exp', 'ctx'), may hold values from -0.125 to 0.125
- weight_up: bfloat16 [8, 2048, 1024], P('exp', 'ctx'), may hold values from -0.125 to 0.125
- weight_down: bfloat16 [8, 1024, 2048], P('exp', None, 'ctx'), may hold values from -0.1875 to 0.1875
- attn_queries: bfloat16 [4096, 2048], P(('ctx', 'exp')), may hold values from -6 to 6
- attn_keys: bfloat16 [4096, 2048], P(('ctx', 'exp')), may hold values from -6 to 6
- grad_out: bfloat16 [4096, 2048], P('ctx', 'exp'), may hold values from -6 to 6
Outputs:
- grad_tokens: bfloat16 [4096, 2048], P(('ctx', 'exp'))
- grad_queries: bfloat16 [4096, 2048], P(('ctx', 'exp'))
- grad_keys: bfloat16 [4096, 2048], P(('ctx', 'exp'))
Inputs may be any that keep to these rules, and one draw needn't show every extreme that they name: `expert_ids`: each row names one expert. Within each aligned block of 128 rows (the rows of one device), no expert is named more than 20 times, a bound that some block reaches.
All inputs are finite; a program needn't handle non-finite values.
Results may differ from a plain program's by a relative error of at most 0.0085.
Values may be sent and summed in bfloat16 or wider, within the bound.
No kernel may reach another device: no remote copies, remote signals or barrier semaphores. Data moves between devices by JAX's collectives and lax.ppermute only.
A program may use at most 64 MiB of HBM per device.

v0:
```python
import math

import jax
import jax.numpy as jnp
from jax import lax
from jax.sharding import PartitionSpec as P

HEAD_DIM = 128
TOPK = 1
BLOCK = 512


def silu_parts(gate_pre):
    sigmoid = jax.nn.sigmoid(gate_pre)
    activation = gate_pre * sigmoid
    silu_slope = sigmoid * (1.0 + gate_pre * (1.0 - sigmoid))
    return (activation, silu_slope)


def expert_move(buffer):
    return lax.all_to_all(buffer, "exp", split_axis=0, concat_axis=0, tiled=True)


def contract_rows(left, right):
    return lax.dot_general(
        left, right, (((1,), (1,)), ((), ())), preferred_element_type=jnp.float32
    )


def block_grads(block_item, attn_scale):
    query_blk, key_blk, value_blk, cot_blk, state_start, state_after = block_item
    length = query_blk.shape[1]
    causal = (jnp.arange(length)[:, None] >= jnp.arange(length)[None, :])[None]
    scores = jnp.where(
        causal,
        jnp.einsum("htd,hsd->hts", query_blk, key_blk, preferred_element_type=jnp.float32),
        0.0,
    ).astype(jnp.bfloat16)
    probes = jnp.where(
        causal,
        jnp.einsum("htv,hsv->hts", cot_blk, value_blk, preferred_element_type=jnp.float32),
        0.0,
    ).astype(jnp.bfloat16)
    start_low = state_start.astype(jnp.bfloat16)
    after_low = state_after.astype(jnp.bfloat16)
    grad_query = attn_scale * (
        jnp.einsum("hts,hsd->htd", probes, key_blk, preferred_element_type=jnp.float32)
        + jnp.einsum("htv,hdv->htd", cot_blk, start_low, preferred_element_type=jnp.float32)
    )
    grad_key = attn_scale * (
        jnp.einsum("hts,htd->hsd", probes, query_blk, preferred_element_type=jnp.float32)
        + jnp.einsum("hsv,hdv->hsd", value_blk, after_low, preferred_element_type=jnp.float32)
    )
    grad_value = attn_scale * (
        jnp.einsum("hts,htv->hsv", scores, cot_blk, preferred_element_type=jnp.float32)
        + jnp.einsum("hsd,hdv->hsv", key_blk, after_low, preferred_element_type=jnp.float32)
    )
    return (
        grad_query.astype(jnp.bfloat16),
        grad_key.astype(jnp.bfloat16),
        grad_value.astype(jnp.bfloat16),
    )


def shards(
    tokens,
    expert_ids,
    gate_weights,
    weight_gate,
    weight_up,
    weight_down,
    attn_queries,
    attn_keys,
    grad_out,
):
    exp_count = lax.axis_size("exp")
    ctx_count = lax.axis_size("ctx")
    row_count, model_width = tokens.shape
    experts = weight_gate.shape[0] * exp_count
    capacity = 5 * row_count * TOPK // (4 * exp_count)
    flat_ids = expert_ids.reshape(-1)
    one_hot = (flat_ids[:, None] == jnp.arange(experts, dtype=jnp.int32)[None, :]).astype(jnp.int32)
    slot_rank = jnp.sum((jnp.cumsum(one_hot, axis=0, dtype=jnp.int32) - one_hot) * one_hot, axis=1)
    slot_dest = flat_ids * capacity + slot_rank
    slot_owner = jnp.arange(row_count * TOPK, dtype=jnp.int32) // TOPK
    slot_source = (
        jnp.full((experts * capacity,), row_count, jnp.int32).at[slot_dest].set(slot_owner)
    )
    dest_table = slot_dest.reshape(row_count, TOPK)
    padded = jnp.concatenate([tokens, jnp.zeros((1, model_width), jnp.bfloat16)], axis=0)
    slot_rows = expert_move(padded[slot_source].reshape(experts, capacity, model_width)).reshape(
        -1, model_width
    )
    full_gate, full_up, full_down = (
        lax.all_gather(weight_gate, "ctx", axis=1, tiled=True),
        lax.all_gather(weight_up, "ctx", axis=1, tiled=True),
        lax.all_gather(weight_down, "ctx", axis=2, tiled=True),
    )
    weight_one = full_gate[0]
    weight_three = full_up[0]
    weight_two = full_down[0]
    gate_pre = jnp.dot(slot_rows, weight_one, preferred_element_type=jnp.float32)
    up_proj = jnp.dot(slot_rows, weight_three, preferred_element_type=jnp.float32)
    activation, silu_slope = silu_parts(gate_pre)
    hidden = (activation * up_proj).astype(jnp.bfloat16)
    expert_out = jnp.dot(hidden, weight_two, preferred_element_type=jnp.float32).astype(
        jnp.bfloat16
    )
    returned = expert_move(expert_out.reshape(exp_count, capacity, model_width)).reshape(
        -1, model_width
    )
    choice_index = 0
    values_sum = gate_weights * returned[dest_table[:, choice_index]].astype(jnp.float32)
    values_mixed = values_sum.astype(jnp.bfloat16)
    part_width = model_width // exp_count
    key_width = max(part_width, HEAD_DIM)
    group_size = key_width // part_width
    local_heads = key_width // HEAD_DIM
    value_width = part_width // local_heads
    span_rows = row_count * exp_count
    attn_scale = 1.0 / math.sqrt(HEAD_DIM * span_rows * ctx_count)
    values_split = jnp.transpose(values_mixed.reshape(row_count, exp_count, part_width), (1, 0, 2))
    query_copies = jnp.repeat(
        jnp.transpose(
            attn_queries.reshape(row_count, model_width // key_width, key_width), (1, 0, 2)
        ),
        group_size,
        axis=0,
    )
    key_copies = jnp.repeat(
        jnp.transpose(attn_keys.reshape(row_count, model_width // key_width, key_width), (1, 0, 2)),
        group_size,
        axis=0,
    )
    value_in, query_in, key_in = (
        lax.all_to_all(values_split, "exp", split_axis=0, concat_axis=0, tiled=True),
        lax.all_to_all(query_copies, "exp", split_axis=0, concat_axis=0, tiled=True),
        lax.all_to_all(key_copies, "exp", split_axis=0, concat_axis=0, tiled=True),
    )
    query_full = query_in.reshape(span_rows, key_width)
    key_full = key_in.reshape(span_rows, key_width)
    nblocks = span_rows // BLOCK

    def to_blocks(flat, width):
        return jnp.transpose(flat.reshape(nblocks, BLOCK, local_heads, width), (0, 2, 1, 3))

    def from_blocks(blocked):
        return jnp.transpose(blocked, (0, 2, 1, 3)).reshape(span_rows, -1)

    query_blocks = to_blocks(query_full, HEAD_DIM)
    key_blocks = to_blocks(key_full, HEAD_DIM)
    value_blocks = to_blocks(value_in.reshape(span_rows, part_width), value_width)
    cot_blocks = to_blocks(grad_out, value_width)
    state_blocks = jnp.einsum(
        "nhbd,nhbv->nhdv", key_blocks, value_blocks, preferred_element_type=jnp.float32
    )
    after_blocks = jnp.einsum(
        "nhbd,nhbv->nhdv", query_blocks, cot_blocks, preferred_element_type=jnp.float32
    )
    state_local = jnp.sum(state_blocks, axis=0)
    after_local = jnp.sum(after_blocks, axis=0)
    every_state, every_after = (
        lax.all_gather(state_local[None], "ctx", axis=0, tiled=True),
        lax.all_gather(after_local[None], "ctx", axis=0, tiled=True),
    )
    position = lax.axis_index("ctx")
    order_ids = jnp.arange(ctx_count, dtype=jnp.int32)
    earlier = (order_ids < position).astype(jnp.float32).reshape(ctx_count, 1, 1, 1)
    later = (order_ids > position).astype(jnp.float32).reshape(ctx_count, 1, 1, 1)
    state_in = jnp.sum(every_state * earlier, axis=0)
    after_in = jnp.sum(every_after * later, axis=0)
    state_start = state_in[None] + jnp.cumsum(state_blocks, axis=0) - state_blocks
    state_after = after_in[None] + after_local[None] - jnp.cumsum(after_blocks, axis=0)

    def run_block(block_item):
        return block_grads(block_item, attn_scale)

    part_query, part_key, part_value = lax.map(
        run_block, (query_blocks, key_blocks, value_blocks, cot_blocks, state_start, state_after)
    )
    value_back = from_blocks(part_value).reshape(exp_count, row_count, part_width)
    flat_query = from_blocks(part_query)
    flat_key = from_blocks(part_key)
    grads_home, query_home, key_home = (
        lax.all_to_all(value_back, "exp", split_axis=0, concat_axis=0, tiled=True),
        lax.all_to_all(
            flat_query.reshape(exp_count, row_count, key_width),
            "exp",
            split_axis=0,
            concat_axis=0,
            tiled=True,
        ),
        lax.all_to_all(
            flat_key.reshape(exp_count, row_count, key_width),
            "exp",
            split_axis=0,
            concat_axis=0,
            tiled=True,
        ),
    )
    query_sum = jnp.sum(
        query_home.reshape(exp_count // group_size, group_size, row_count, key_width).astype(
            jnp.float32
        ),
        axis=1,
    ).astype(jnp.bfloat16)
    key_sum = jnp.sum(
        key_home.reshape(exp_count // group_size, group_size, row_count, key_width).astype(
            jnp.float32
        ),
        axis=1,
    ).astype(jnp.bfloat16)
    grad_queries = jnp.transpose(query_sum, (1, 0, 2)).reshape(row_count, model_width)
    grad_keys = jnp.transpose(key_sum, (1, 0, 2)).reshape(row_count, model_width)
    grads_mixed = jnp.transpose(grads_home, (1, 0, 2)).reshape(row_count, model_width)
    padded_grads = jnp.concatenate([grads_mixed, jnp.zeros((1, model_width), jnp.bfloat16)], axis=0)
    slot_grads = expert_move(
        padded_grads[slot_source].reshape(experts, capacity, model_width)
    ).reshape(-1, model_width)
    grad_hidden = contract_rows(slot_grads, weight_two)
    grad_gate = (grad_hidden * up_proj * silu_slope).astype(jnp.bfloat16)
    grad_up = (grad_hidden * activation).astype(jnp.bfloat16)
    expert_grad = (
        contract_rows(grad_gate, weight_one) + contract_rows(grad_up, weight_three)
    ).astype(jnp.bfloat16)
    grad_home = expert_move(expert_grad.reshape(exp_count, capacity, model_width)).reshape(
        -1, model_width
    )
    choice_index = 0
    grad_sum = gate_weights * grad_home[dest_table[:, choice_index]].astype(jnp.float32)
    grad_tokens = grad_sum.astype(jnp.bfloat16)
    return (grad_tokens, grad_queries, grad_keys)


def solution(mesh):
    in_specs = (
        P(("ctx", "exp"), None),
        P(("ctx", "exp"), None),
        P(("ctx", "exp"), None),
        P("exp", "ctx", None),
        P("exp", "ctx", None),
        P("exp", None, "ctx"),
        P(("ctx", "exp"), None),
        P(("ctx", "exp"), None),
        P("ctx", "exp"),
    )
    out_specs = (P(("ctx", "exp"), None), P(("ctx", "exp"), None), P(("ctx", "exp"), None))
    return jax.shard_map(shards, mesh=mesh, in_specs=in_specs, out_specs=out_specs, check_vma=False)
```

profile of v0, /device:TPU:0, one launch (start us, length us, event | category | flops | bytes accessed | tf_op | source)
XLA Modules:
  0.0 423.5 jit_solution(16311759220426630316)
XLA Ops:
  14.8 5.2 %all-to-all-start = ((bf16[8,20,2048]{2,1,0:T(8,128)(2,1)}), bf16[8,20,2048]{2,1,0:T(8,128)(2,1)S(1)}, u32[]{:S(2)}, u32[]{:S(2)}) async-start(bf16[8,20,2048]{2,1,0:T(8,128)(2,1)} %reshape.101), calls=%async_computation | async-start | bytes 1572864 | tf_op jit(solution)/shard_map/all_to_all | solution.py:21
  20.8 11.8 %all-to-all-done = bf16[8,20,2048]{2,1,0:T(8,128)(2,1)S(1)} async-done(((bf16[8,20,2048]{2,1,0:T(8,128)(2,1)}), bf16[8,20,2048]{2,1,0:T(8,128)(2,1)S(1)}, u32[]{:S(2)}, u32[]{:S(2)}) %all-to-all-start) | async-done | bytes 655392 | tf_op jit(solution)/shard_map/all_to_all | solution.py:21
  32.5 3.5 all-to-all-start.4
  36.2 56.9 %all-gather.6.cloned.1.call-done = bf16[1,2048,1024]{2,1,0:T(8,128)(2,1)} async-done(((bf16[1,512,1024]{2,1,0:T(8,128)(2,1)}), bf16[1,2048,1024]{2,1,0:T(8,128)(2,1)}) %all-gather.6.cloned.1.call-update) | async-done | bytes 4194320 | tf_op jit(solution)/shard_map/all_gather | solution.py:95
  93.1 3.0 fusion.67
  96.1 77.8 %all-gather.8.cloned.1.call-done = bf16[1,2048,1024]{2,1,0:T(8,128)(2,1)} async-done(((bf16[1,512,1024]{2,1,0:T(8,128)(2,1)}), bf16[1,2048,1024]{2,1,0:T(8,128)(2,1)}) %all-gather.8.cloned.1.call-update) | async-done | bytes 4194320 | tf_op jit(solution)/shard_map/all_gather | solution.py:96
  174.0 3.0 fusion.63
  177.0 77.8 %all-gather.10.cloned.1.call-done = bf16[1,1024,2048]{2,1,0:T(8,128)(2,1)} async-done(((bf16[1,1024,512]{2,1,0:T(8,128)(2,1)}), bf16[1,1024,2048]{2,1,0:T(8,128)(2,1)}) %all-gather.10.cloned.1.call-update) | async-done | bytes 4194320 | tf_op jit(solution)/shard_map/all_gather | solution.py:97
  254.9 3.1 fusion.72
  259.0 3.7 all-to-all-start.1
  265.9 9.4 %all-to-all-done.1 = bf16[8,20,2048]{2,1,0:T(8,128)(2,1)S(1)} async-done(((bf16[8,20,2048]{2,1,0:T(8,128)(2,1)}), bf16[8,20,2048]{2,1,0:T(8,128)(2,1)S(1)}, u32[]{:S(2)}, u32[]{:S(2)}) %all-to-all-start.1) | async-done | bytes 655392 | tf_op jit(solution)/shard_map/all_to_all | solution.py:21
  275.3 3.5 all-to-all-start.3
  278.8 1.7 fusion.97
  282.6 5.8 %all-to-all-done.3 = bf16[8,128,256]{2,1,0:T(8,128)(2,1)S(1)} async-done(((bf16[8,128,256]{2,1,0:T(8,128)(2,1)}), bf16[8,128,256]{2,1,0:T(8,128)(2,1)S(1)}, u32[]{:S(2)}, u32[]{:S(2)}) %all-to-all-start.3) | async-done | bytes 524320 | tf_op jit(solution)/shard_map/all_to_all | solution.py:138
  288.5 3.5 all-to-all-start.2
  292.0 16.2 %all-gather.1 = f32[8,128,128]{2,1,0:T(8,128)S(1)} all-gather(f32[2,128,128]{2,1,0:T(8,128)S(1)} %copy-done.1), channel_id=3, replica_groups=mesh['ctx'=4,'exp'=8] {'ctx'}, dimensions={0}, use_global_device_ids=true | all-gather | bytes 655360 | tf_op jit(solution)/shard_map/all_gather | solution.py:164
  312.9 14.8 %all-gather = f32[8,128,128]{2,1,0:T(8,128)S(1)} all-gather(f32[2,128,128]{2,1,0:T(8,128)S(1)} %copy.83), channel_id=2, replica_groups=mesh['ctx'=4,'exp'=8] {'ctx'}, dimensions={0}, use_global_device_ids=true | all-gather | bytes 655360 | tf_op jit(solution)/shard_map/all_gather | solution.py:163
  328.0 10.7 %while.14 = (s32[]{:T(128)}, bf16[2,2,512,128]{3,2,1,0:T(8,128)(2,1)}, bf16[2,2,512,128]{3,2,1,0:T(8,128)(2,1)}, bf16[2,2,512,128]{3,2,1,0:T(8,128)(2,1)}, bf16[...) while((s32[]{:T(128)}, ...), condition=%wide.region_10.11_spmd, body=%wide.region_9.10_spmd.sunk | while | flops 775290880 | bytes 10951797 | solution.py:178
  338.6 1.6 copy.92
  340.6 13.6 %all_to_all.50 = bf16[8,128,256]{2,1,0:T(8,128)(2,1)S(1)} all-to-all(bf16[8,128,256]{2,1,0:T(8,128)(2,1)S(1)} %reshape_reshape.21), channel_id=1, replica_groups=mesh['ctx'=4,'exp'=8] {'exp'}, dimensions={0} | all-to-all | bytes 1048576 | tf_op jit(solution)/shard_map/all_to_all | solution.py:185
  356.5 3.5 all-to-all-start.6
  361.7 1.6 copy.96
  364.4 8.1 %all-to-all-done.6 = bf16[8,20,2048]{2,1,0:T(8,128)(2,1)S(1)} async-done(((bf16[8,20,2048]{2,1,0:T(8,128)(2,1)}), bf16[8,20,2048]{2,1,0:T(8,128)(2,1)S(1)}, u32[]{:S(2)}, u32[]{:S(2)}) %all-to-all-start.6) | async-done | bytes 655392 | tf_op jit(solution)/shard_map/all_to_all | solution.py:21
  372.5 3.5 all-to-all-start.8
  376.2 3.9 fusion.57
  381.0 2.7 fusion.61
  383.6 2.1 all-to-all-done.8
  385.7 3.5 all-to-all-start.9
  389.2 4.3 %fusion.75 = bf16[160,2048]{1,0:T(8,128)(2,1)S(1)} fusion(f32[160,2048]{1,0:T(8,128)} %fusion.61, bf16[1,2048,1024]{2,1,0:T(8,128)(2,1)} %all-gather.6.cloned.1.call-done, f32[160,1024]{1,0:T(8,128)S(1)} %copy-done.4, f32[160,1024]{1,0:T(8,128)} %copy-done.7, f32[160,1024]{1,0:T(8,128)S(1)} %copy-done.6), kind=kOutput, calls=%fused_computation.76 | convolution fusion | flops 673382400 | bytes 8126464 | tf_op jit(solution)/shard_map/dot_general | solution.py:25
  394.6 4.3 %all-to-all-done.9 = bf16[8,128,256]{2,1,0:T(8,128)(2,1)S(1)} async-done(((bf16[8,128,256]{2,1,0:T(8,128)(2,1)}), bf16[8,128,256]{2,1,0:T(8,128)(2,1)S(1)}, u32[]{:S(2)}, u32[]{:S(2)}) %all-to-all-start.9) | async-done | bytes 524320 | tf_op jit(solution)/shard_map/all_to_all | solution.py:193
  398.9 3.5 all-to-all-start.7
  405.0 10.0 %all-to-all-done.7 = bf16[8,20,2048]{2,1,0:T(8,128)(2,1)S(1)} async-done(((bf16[8,20,2048]{2,1,0:T(8,128)(2,1)}), bf16[8,20,2048]{2,1,0:T(8,128)(2,1)S(1)}, u32[]{:S(2)}, u32[]{:S(2)}) %all-to-all-start.7) | async-done | bytes 655392 | tf_op jit(solution)/shard_map/all_to_all | solution.py:21
  (116 shorter events, 42.4 us)
Async XLA Ops:
  7.2 4.2 %copy-start.11 = (s32[128,1]{0,1:T(1,128)S(1)}, s32[128,1]{0,1:T(1,128)}, u32[]{:S(2)}) copy-start(s32[128,1]{0,1:T(1,128)} %param.12) | copy-start | bytes 1540
  7.2 85.9 %all-gather.6.cloned.1.call-start = ((), (), s32[]{:S(2)}) async-start(), calls=%async_computation.10 | async-start | bytes 5242880 | tf_op jit(solution)/shard_map/all_gather | solution.py:95
  7.9 166.1 %all-gather.8.cloned.1.call-start = ((), (), s32[]{:S(2)}) async-start(), calls=%async_computation.11 | async-start | bytes 5242880 | tf_op jit(solution)/shard_map/all_gather | solution.py:96
  8.7 246.2 %all-gather.10.cloned.1.call-start = ((), (), s32[]{:S(2)}) async-start(), calls=%async_computation.12 | async-start | bytes 5242880 | tf_op jit(solution)/shard_map/all_gather | solution.py:97
  12.6 7.3 %copy-start.8 = (bf16[128,2048]{1,0:T(8,128)(2,1)S(1)}, bf16[128,2048]{1,0:T(8,128)(2,1)}, u32[]{:S(2)}) copy-start(bf16[128,2048]{1,0:T(8,128)(2,1)} %param.17) | copy-start | bytes 1572868
  14.8 17.8 %all-to-all-start = ((bf16[8,20,2048]{2,1,0:T(8,128)(2,1)}), bf16[8,20,2048]{2,1,0:T(8,128)(2,1)S(1)}, u32[]{:S(2)}, u32[]{:S(2)}) async-start(bf16[8,20,2048]{2,1,0:T(8,128)(2,1)} %reshape.101), calls=%async_computation | async-start | bytes 1572864 | tf_op jit(solution)/shard_map/all_to_all | solution.py:21
  32.5 226.5 %all-to-all-start.4 = ((bf16[8,128,256]{2,1,0:T(8,128)(2,1)}), bf16[8,128,256]{2,1,0:T(8,128)(2,1)S(1)}, u32[]{:S(2)}, u32[]{:S(2)}) async-start(bf16[8,128,256]{2,1,0:T(8,128)(2,1)} %bitcast.135), calls=%async_computation.4 | async-start | bytes 1048576 | tf_op jit(solution)/shard_map/all_to_all | solution.py:137
  96.1 161.8 %copy-start.3 = (f32[160,1024]{1,0:T(8,128)}, f32[160,1024]{1,0:T(8,128)S(1)}, u32[]{:S(2)}) copy-start(f32[160,1024]{1,0:T(8,128)S(1)} %fusion.67) | copy-start | bytes 1966084
  177.0 82.0 %copy-start.5 = (f32[160,1024]{1,0:T(8,128)}, f32[160,1024]{1,0:T(8,128)S(1)}, u32[]{:S(2)}) copy-start(f32[160,1024]{1,0:T(8,128)S(1)} %fusion.63) | copy-start | bytes 1966084
  177.0 85.7 %copy-start.9 = (bf16[128,2048]{1,0:T(8,128)(2,1)S(1)}, bf16[128,2048]{1,0:T(8,128)(2,1)}, u32[]{:S(2)}) copy-start(bf16[128,2048]{1,0:T(8,128)(2,1)} %param.18) | copy-start | bytes 1572868
  259.0 16.3 %all-to-all-start.1 = ((bf16[8,20,2048]{2,1,0:T(8,128)(2,1)}), bf16[8,20,2048]{2,1,0:T(8,128)(2,1)S(1)}, u32[]{:S(2)}, u32[]{:S(2)}) async-start(bf16[8,20,2048]{2,1,0:T(8,128)(2,1)} %reshape.103), calls=%async_computation.1 | async-start | bytes 1572864 | tf_op jit(solution)/shard_map/all_to_all | solution.py:21
  275.3 13.2 %all-to-all-start.3 = ((bf16[8,128,256]{2,1,0:T(8,128)(2,1)}), bf16[8,128,256]{2,1,0:T(8,128)(2,1)S(1)}, u32[]{:S(2)}, u32[]{:S(2)}) async-start(bf16[8,128,256]{2,1,0:T(8,128)(2,1)} %bitcast.137), calls=%async_computation.3 | async-start | bytes 1048576 | tf_op jit(solution)/shard_map/all_to_all | solution.py:138
  280.5 1.2 copy-start.12
  280.6 11.4 %copy-start.1 = (f32[2,128,128]{2,1,0:T(8,128)S(1)}, f32[2,128,128]{2,1,0:T(8,128)}, u32[]{:S(2)}) copy-start(f32[2,128,128]{2,1,0:T(8,128)} %get-tuple-element.141) | copy-start | bytes 393220
  280.6 27.6 %copy-start.13 = (f32[4]{0:T(128)S(1)}, f32[4]{0:T(128)}, u32[]{:S(2)}) copy-start(f32[4]{0:T(128)} %compare_convert_fusion) | copy-start | bytes 52
  281.6 27.7 %copy-start.2 = (f32[2,2,128,128]{3,2,1,0:T(8,128)S(1)}, f32[2,2,128,128]{3,2,1,0:T(8,128)}, u32[]{:S(2)}) copy-start(f32[2,2,128,128]{3,2,1,0:T(8,128)} %get-tuple-element.142) | copy-start | bytes 786436
  288.5 21.7 %all-to-all-start.2 = ((bf16[8,128,256]{2,1,0:T(8,128)(2,1)}), bf16[8,128,256]{2,1,0:T(8,128)(2,1)S(1)}, u32[]{:S(2)}, u32[]{:S(2)}) async-start(bf16[8,128,256]{2,1,0:T(8,128)(2,1)} %fusion.81), calls=%async_computation.2 | async-start | bytes 1048576 | tf_op jit(solution)/shard_map/all_to_all | solution.py:136
  354.3 5.7 %copy-start.10 = (bf16[2,2,512,128]{3,2,1,0:T(8,128)(2,1)S(1)}, bf16[2,2,512,128]{3,2,1,0:T(8,128)(2,1)}, u32[]{:S(2)}) copy-start(bf16[2,2,512,128]{3,2,1,0:T(8,128)(2,1)} %get-tuple-element.58) | copy-start | bytes 1572868
  356.5 16.1 %all-to-all-start.6 = ((bf16[8,20,2048]{2,1,0:T(8,128)(2,1)}), bf16[8,20,2048]{2,1,0:T(8,128)(2,1)S(1)}, u32[]{:S(2)}, u32[]{:S(2)}) async-start(bf16[8,20,2048]{2,1,0:T(8,128)(2,1)} %reshape.108), calls=%async_computation.6 | async-start | bytes 1572864 | tf_op jit(solution)/shard_map/all_to_all | solution.py:21
  364.4 16.6 %copy-start.4 = (f32[160,1024]{1,0:T(8,128)S(1)}, f32[160,1024]{1,0:T(8,128)}, u32[]{:S(2)}) copy-start(f32[160,1024]{1,0:T(8,128)} %copy-done.3) | copy-start | bytes 1966084
  372.5 13.2 %all-to-all-start.8 = ((bf16[8,128,256]{2,1,0:T(8,128)(2,1)}), bf16[8,128,256]{2,1,0:T(8,128)(2,1)S(1)}, u32[]{:S(2)}, u32[]{:S(2)}) async-start(bf16[8,128,256]{2,1,0:T(8,128)(2,1)} %reshape_reshape.22), calls=%async_computation.8 | async-start | bytes 1048576 | tf_op jit(solution)/shard_map/all_to_all | solution.py:186
  376.2 4.8 %copy-start = (bf16[1,2048,1024]{2,1,0:T(8,128)(2,1)S(1)}, bf16[1,2048,1024]{2,1,0:T(8,128)(2,1)}, u32[]{:S(2)}) copy-start(bf16[1,2048,1024]{2,1,0:T(8,128)(2,1)} %all-gather.8.cloned.1.call-done) | copy-start | bytes 12582916
  380.1 0.9 copy-start.7
  381.0 8.2 %copy-start.6 = (f32[160,1024]{1,0:T(8,128)S(1)}, f32[160,1024]{1,0:T(8,128)}, u32[]{:S(2)}) copy-start(f32[160,1024]{1,0:T(8,128)} %copy-done.5) | copy-start | bytes 1966084
  385.7 13.2 %all-to-all-start.9 = ((bf16[8,128,256]{2,1,0:T(8,128)(2,1)}), bf16[8,128,256]{2,1,0:T(8,128)(2,1)S(1)}, u32[]{:S(2)}, u32[]{:S(2)}) async-start(bf16[8,128,256]{2,1,0:T(8,128)(2,1)} %reshape_reshape.23), calls=%async_computation.9 | async-start | bytes 1048576 | tf_op jit(solution)/shard_map/all_to_all | solution.py:193
  398.9 16.1 %all-to-all-start.7 = ((bf16[8,20,2048]{2,1,0:T(8,128)(2,1)}), bf16[8,20,2048]{2,1,0:T(8,128)(2,1)S(1)}, u32[]{:S(2)}, u32[]{:S(2)}) async-start(bf16[8,20,2048]{2,1,0:T(8,128)(2,1)} %reshape.110), calls=%async_computation.7 | async-start | bytes 1572864 | tf_op jit(solution)/shard_map/all_to_all | solution.py:21
Sparse Core Ops, SparseCore 0:
  9.6 83.4 all-gather.5
  94.6 79.2 all-gather.7
  175.5 79.2 all-gather.9
where the time goes:
time: 425 us; the launch traced here: 424 us
  waiting for transfers between devices  266 us (63%)
  blocking collectives  44.5 us (10%)
  starting transfers between devices  33.5 us (8%)
  matrix products  33.2 us (8%)
  local copies, waits for them, and re-layouts  26.2 us (6%)
  between operations  14.3 us (3%)
  other arithmetic  5.63 us (1%)
    all_gather x1, waiting for transfers between devices, shards(): lax.all_gather(weight_up, 'ctx', axis=1, tiled=True)  77.8 us
    all_gather x1, waiting for transfers between devices, shards(): lax.all_gather(weight_down, 'ctx', axis=2, tiled=True)  77.8 us
    all_gather x1, waiting for transfers between devices, shards(): lax.all_gather(weight_gate, 'ctx', axis=1, tiled=True)  56.9 us
    all_to_all x4, waiting for transfers between devices, expert_move(): lax.all_to_all(buffer, 'exp', split_axis=0, concat_axis=0, tiled=True)  39.3 us
    all_gather x1, blocking collectives, shards(): lax.all_gather(after_local[None], 'ctx', axis=0, tiled=True)  16.2 us
    all_to_all x4, starting transfers between devices, expert_move(): lax.all_to_all(buffer, 'exp', split_axis=0, concat_axis=0, tiled=True)  15.9 us
    all_gather x1, blocking collectives, shards(): lax.all_gather(state_local[None], 'ctx', axis=0, tiled=True)  14.8 us
    all_to_all x1, blocking collectives, shards(): lax.all_to_all(value_back, 'exp', split_axis=0, concat_axis=0, tiled=True)  13.6 us
  transfers between devices with their start and end apart: 12, of which 10 were waited for; matrix products, arithmetic and copies ran while one was open for 10% of the time, Pallas kernels for 0%

commit v1 on v0

v1 whole, which is shorter than its diff:
```python
import math

import jax
import jax.numpy as jnp
from jax import lax
from jax.sharding import PartitionSpec as P

HEAD_DIM = 128
TOPK = 1
BLOCK = 512


def silu_parts(gate_pre):
    sigmoid = jax.nn.sigmoid(gate_pre)
    activation = gate_pre * sigmoid
    silu_slope = sigmoid * (1.0 + gate_pre * (1.0 - sigmoid))
    return (activation, silu_slope)


def dot(left, right):
    return jnp.dot(left, right, preferred_element_type=jnp.float32)


def contract_rows(left, right):
    return lax.dot_general(
        left, right, (((1,), (1,)), ((), ())), preferred_element_type=jnp.float32
    )


def contract_first(left, right):
    return lax.dot_general(
        left, right, (((0,), (0,)), ((), ())), preferred_element_type=jnp.float32
    )


def move(buffer, axes):
    return lax.all_to_all(buffer, axes, split_axis=0, concat_axis=0, tiled=True)


def swap(block, axis, distance):
    count = lax.axis_size(axis)
    return lax.ppermute(block, axis, [(i, i ^ distance) for i in range(count)])


def pick(blocks, index):
    return lax.dynamic_index_in_dim(blocks, index, 0, keepdims=False)


def reduce_to_owner(blocks, axis):
    count = lax.axis_size(axis)
    me = lax.axis_index(axis)
    held = {offset: pick(blocks, me ^ offset) for offset in range(count)}
    distance = 1
    while distance < count:
        sent = sorted((o for o in held if o & distance), reverse=True)
        arrived = {o ^ distance: swap(held[o].astype(jnp.bfloat16), axis, distance) for o in sent}
        held = {o: held[o] + arrived[o].astype(jnp.float32) for o in held if not o & distance}
        distance *= 2
    return held[0]


def gather_by_offset(block, axis):
    count = lax.axis_size(axis)
    held = {0: block}
    distance = count // 2
    while distance:
        held.update({o | distance: swap(b, axis, distance) for o, b in list(held.items())})
        distance //= 2
    return held


def shards(
    tokens,
    expert_ids,
    gate_weights,
    weight_gate,
    weight_up,
    weight_down,
    attn_queries,
    attn_keys,
    grad_out,
):
    exp_count = lax.axis_size("exp")
    ctx_count = lax.axis_size("ctx")
    row_count, model_width = tokens.shape
    hidden_width = weight_gate.shape[2]
    slice_width = weight_gate.shape[1]
    experts = weight_gate.shape[0] * exp_count
    capacity = 5 * row_count * TOPK // (4 * exp_count)
    slots = experts * capacity
    part_width = model_width // exp_count
    key_width = max(part_width, HEAD_DIM)
    group_size = key_width // part_width
    local_heads = key_width // HEAD_DIM
    value_width = part_width // local_heads
    span_rows = row_count * exp_count
    nblocks = span_rows // BLOCK
    attn_scale = 1.0 / math.sqrt(HEAD_DIM * span_rows * ctx_count)

    weight_two = lax.all_gather(weight_down[0], "ctx", axis=1, tiled=True)

    flat_ids = expert_ids.reshape(-1)
    one_hot = flat_ids[:, None] == jnp.arange(experts, dtype=jnp.int32)[None, :]
    row_ids = jnp.arange(row_count, dtype=jnp.int32)
    before = (row_ids[None, :] < row_ids[:, None]).astype(jnp.bfloat16)
    counts = dot(before, one_hot.astype(jnp.bfloat16))
    slot_rank = jnp.sum(jnp.where(one_hot, counts, 0.0), axis=1).astype(jnp.int32)
    slot_dest = flat_ids * capacity + slot_rank
    dispatch = (jnp.arange(slots, dtype=jnp.int32)[:, None] == slot_dest[None, :]).astype(jnp.bfloat16)
    slot_rows = dot(dispatch, tokens).astype(jnp.bfloat16)
    outgoing = jnp.transpose(
        slot_rows.reshape(experts, capacity, ctx_count, slice_width), (2, 0, 1, 3)
    ).reshape(ctx_count * experts, capacity, slice_width)
    incoming = move(outgoing, ("ctx", "exp")).reshape(ctx_count * slots, slice_width)

    me = lax.axis_index("exp")
    place = flat_ids * slots + me * capacity + slot_rank
    info = jnp.concatenate(
        [place.astype(jnp.float32)[None], gate_weights.reshape(1, -1), jnp.zeros((6, row_count), jnp.float32)]
    )
    info = move(jnp.broadcast_to(info[None], (exp_count, 8, row_count)), "exp")
    span_place = info[:, 0].reshape(span_rows).astype(jnp.int32)
    span_gate = info[:, 1].reshape(span_rows, 1)
    spread = (
        span_place[:, None] == jnp.arange(experts * slots, dtype=jnp.int32)[None, :]
    ).astype(jnp.bfloat16)

    def heads_in(array):
        copies = jnp.repeat(
            jnp.transpose(array.reshape(row_count, model_width // key_width, key_width), (1, 0, 2)),
            group_size,
            axis=0,
        )
        return move(copies, "exp").reshape(span_rows, key_width)

    def to_blocks(flat, width):
        return jnp.transpose(flat.reshape(nblocks, BLOCK, local_heads, width), (0, 2, 1, 3))

    def from_blocks(blocked):
        return jnp.transpose(blocked, (0, 2, 1, 3)).reshape(span_rows, -1)

    query_blocks = to_blocks(heads_in(attn_queries), HEAD_DIM)
    key_blocks = to_blocks(heads_in(attn_keys), HEAD_DIM)
    cot_blocks = to_blocks(grad_out, value_width)

    partial = jnp.concatenate(
        [dot(incoming, weight_gate[0]), dot(incoming, weight_up[0])], axis=1
    )
    projected = reduce_to_owner(partial.reshape(ctx_count, slots, 2 * hidden_width), "ctx")
    gate_pre, up_proj = projected[:, :hidden_width], projected[:, hidden_width:]
    activation, silu_slope = silu_parts(gate_pre)

    causal = jnp.arange(BLOCK)[:, None] >= jnp.arange(BLOCK)[None, :]
    after_blocks = jnp.einsum(
        "nhbd,nhbv->nhdv", query_blocks, cot_blocks, preferred_element_type=jnp.float32
    )
    after_local = jnp.sum(after_blocks, axis=0)
    state_after = after_local[None] - jnp.cumsum(after_blocks, axis=0)
    for step in range(1, ctx_count):
        state_after = state_after + lax.ppermute(
            after_local, "ctx", [(i + step, i) for i in range(ctx_count - step)]
        )
    after_low = state_after.astype(jnp.bfloat16)
    scores = jnp.where(
        causal,
        jnp.einsum("nhtd,nhsd->nhts", query_blocks, key_blocks, preferred_element_type=jnp.float32),
        0.0,
    ).astype(jnp.bfloat16)
    grad_values = (
        attn_scale
        * (
            jnp.einsum("nhts,nhtv->nhsv", scores, cot_blocks, preferred_element_type=jnp.float32)
            + jnp.einsum("nhsd,nhdv->nhsv", key_blocks, after_low, preferred_element_type=jnp.float32)
        )
    ).astype(jnp.bfloat16)
    slot_grads = contract_first(spread, from_blocks(grad_values)).astype(jnp.bfloat16)
    slot_grads = move(slot_grads.reshape(exp_count, slots, part_width), "exp")
    slot_grads = jnp.transpose(slot_grads, (1, 0, 2)).reshape(slots, model_width)

    hidden = (activation * up_proj).astype(jnp.bfloat16)
    expert_out = dot(hidden, weight_two).astype(jnp.bfloat16)
    returned = move(
        jnp.transpose(expert_out.reshape(slots, exp_count, part_width), (1, 0, 2)), "exp"
    ).reshape(experts * slots, part_width)
    values = (span_gate * dot(spread, returned)).astype(jnp.bfloat16)

    grad_hidden = contract_rows(slot_grads, weight_two)
    grad_both = jnp.concatenate(
        [grad_hidden * up_proj * silu_slope, grad_hidden * activation], axis=1
    ).astype(jnp.bfloat16)
    home = jnp.zeros((ctx_count, slots, slice_width), jnp.bfloat16)
    for offset, block in gather_by_offset(grad_both, "ctx").items():
        expert_grad = (
            contract_rows(block[:, :hidden_width], weight_gate[0])
            + contract_rows(block[:, hidden_width:], weight_up[0])
        ).astype(jnp.bfloat16)
        home = lax.dynamic_update_index_in_dim(home, expert_grad, lax.axis_index("ctx") ^ offset, 0)
    home = move(home.reshape(ctx_count * experts, capacity, slice_width), ("ctx", "exp"))
    home = jnp.transpose(home.reshape(ctx_count, slots, slice_width), (1, 0, 2)).reshape(slots, model_width)
    grad_tokens = (gate_weights * contract_first(dispatch, home)).astype(jnp.bfloat16)

    value_blocks = to_blocks(values, value_width)
    state_blocks = jnp.einsum(
        "nhbd,nhbv->nhdv", key_blocks, value_blocks, preferred_element_type=jnp.float32
    )
    state_local = jnp.sum(state_blocks, axis=0)
    state_start = jnp.cumsum(state_blocks, axis=0) - state_blocks
    for step in range(1, ctx_count):
        state_start = state_start + lax.ppermute(
            state_local, "ctx", [(i, i + step) for i in range(ctx_count - step)]
        )
    start_low = state_start.astype(jnp.bfloat16)
    probes = jnp.where(
        causal,
        jnp.einsum("nhtv,nhsv->nhts", cot_blocks, value_blocks, preferred_element_type=jnp.float32),
        0.0,
    ).astype(jnp.bfloat16)
    part_query = attn_scale * (
        jnp.einsum("nhts,nhsd->nhtd", probes, key_blocks, preferred_element_type=jnp.float32)
        + jnp.einsum("nhtv,nhdv->nhtd", cot_blocks, start_low, preferred_element_type=jnp.float32)
    )
    part_key = attn_scale * (
        jnp.einsum("nhts,nhtd->nhsd", probes, query_blocks, preferred_element_type=jnp.float32)
        + jnp.einsum("nhsv,nhdv->nhsd", value_blocks, after_low, preferred_element_type=jnp.float32)
    )

    def heads_out(part):
        back = move(
            from_blocks(part.astype(jnp.bfloat16)).reshape(exp_count, row_count, key_width), "exp"
        )
        if group_size > 1:
            back = jnp.sum(
                back.reshape(exp_count // group_size, group_size, row_count, key_width).astype(jnp.float32),
                axis=1,
            ).astype(jnp.bfloat16)
        return jnp.transpose(back, (1, 0, 2)).reshape(row_count, model_width)

    return (grad_tokens, heads_out(part_query), heads_out(part_key))


def solution(mesh):
    in_specs = (
        P(("ctx", "exp"), None),
        P(("ctx", "exp"), None),
        P(("ctx", "exp"), None),
        P("exp", "ctx", None),
        P("exp", "ctx", None),
        P("exp", None, "ctx"),
        P(("ctx", "exp"), None),
        P(("ctx", "exp"), None),
        P("ctx", "exp"),
    )
    out_specs = (P(("ctx", "exp"), None), P(("ctx", "exp"), None), P(("ctx", "exp"), None))
    return jax.shard_map(shards, mesh=mesh, in_specs=in_specs, out_specs=out_specs, check_vma=False)
```

time: 425 us -> 273 us (0.64)
  waiting for transfers between devices: 266 us -> 119 us
  blocking collectives: 44.5 us -> 0 us
  starting transfers between devices: 33.5 us -> 57.1 us
  matrix products: 33.2 us -> 42.7 us
  other arithmetic: 5.63 us -> 10.7 us
    all_gather x3 -> x1, waiting for transfers between devices: 213 us -> 0.01 us  [shards(): weight_two = lax.all_gather(weight_down[0], 'ctx', axis=1, tiled=True)]
    all_to_all x9, waiting for transfers between devices: 51.5 us -> 87.2 us  [move(): return lax.all_to_all(buffer, axes, split_axis=0, concat_axis=0, tiled=True)]
    ppermute x0 -> x12, waiting for transfers between devices: none -> 31 us  [the longest x6 30.5 us: swap(): return lax.ppermute(block, axis, [(i, i ^ distance) for i in range(count)])]
    all_gather x2 -> x0, blocking collectives: 30.9 us -> none  [the longest x1 16.2 us: shards(): lax.all_gather(after_local[None], 'ctx', axis=0, tiled=True)]
    ppermute x0 -> x12, starting transfers between devices: none -> 19.5 us  [the longest x3 8.24 us: shards(): lax.ppermute(state_local, 'ctx', [(i, i + step) for i in range(ctx_count...]
    all_to_all x1 -> x0, blocking collectives: 13.6 us -> none  [shards(): lax.all_to_all(value_back, 'exp', split_axis=0, concat_axis=0, tiled=True)]
    dot_general x3 -> x9, matrix products: 10.9 us -> 17 us  [contract_rows(): lax.dot_general(left, right, (((1,), (1,)), ((), ())), preferred_element_...]
    dot_general x17 -> x15, matrix products: 19.3 us -> 24.3 us  [the longest x6 9.35 us: dot(): return jnp.dot(left, right, preferred_element_type=jnp.float32)]
  transfers between devices with their start and end apart: 12 -> 22, of which waited for: 10 -> 12; matrix products, arithmetic and copies ran while one was open for 10% -> 27% of each run, Pallas kernels for 0% -> 0%
where the time goes in v1:
time: 273 us; the launch traced here: 271 us
  waiting for transfers between devices  119 us (44%)
  starting transfers between devices  57.1 us (21%)
  matrix products  42.7 us (16%)
  local copies, waits for them, and re-layouts  27.5 us (10%)
  between operations  14.6 us (5%)
  other arithmetic  10.7 us (4%)
    all_to_all x9, waiting for transfers between devices, move(): return lax.all_to_all(buffer, axes, split_axis=0, concat_axis=0, tiled=True)  87.2 us
    all_to_all x9, starting transfers between devices, move(): return lax.all_to_all(buffer, axes, split_axis=0, concat_axis=0, tiled=True)  37.6 us
    ppermute x6, waiting for transfers between devices, swap(): return lax.ppermute(block, axis, [(i, i ^ distance) for i in range(count)])  30.5 us
    dot_general x9, matrix products, contract_rows(): lax.dot_general(left, right, (((1,), (1,)), ((), ())), preferred_element_...  17 us
    dot_general x6, matrix products, dot(): return jnp.dot(left, right, preferred_element_type=jnp.float32)  9.35 us
    ppermute x3, starting transfers between devices, shards(): lax.ppermute(state_local, 'ctx', [(i, i + step) for i in range(ctx_count...  8.24 us
    ppermute x6, starting transfers between devices, swap(): return lax.ppermute(block, axis, [(i, i ^ distance) for i in range(count)])  7.43 us
  transfers between devices with their start and end apart: 22, of which 12 were waited for; matrix products, arithmetic and copies ran while one was open for 27% of the time, Pallas kernels for 0%

profile of v1, /device:TPU:0, one launch (start us, length us, event | category | flops | bytes accessed | tf_op | source)
XLA Modules:
  0.0 271.5 jit_solution(9250327954235348614)
XLA Ops:
  10.9 5.2 %all-to-all-start = ((f32[8,8,128]{2,1,0:T(8,128)}), f32[8,8,128]{2,1,0:T(8,128)S(1)}, u32[]{:S(2)}, u32[]{:S(2)}) async-start(f32[8,8,128]{2,1,0:T(8,128)} %broadcast_in_dim.61), calls=%async_computation | async-start | bytes 65536 | tf_op jit(solution)/shard_map/all_to_all | solution.py:37
  18.0 2.9 %all-to-all-done = f32[8,8,128]{2,1,0:T(8,128)S(1)} async-done(((f32[8,8,128]{2,1,0:T(8,128)}), f32[8,8,128]{2,1,0:T(8,128)S(1)}, u32[]{:S(2)}, u32[]{:S(2)}) %all-to-all-start) | async-done | bytes 32800 | tf_op jit(solution)/shard_map/all_to_all | solution.py:37
  20.9 3.5 %all-to-all-start.1 = ((bf16[8,128,256]{2,1,0:T(8,128)(2,1)}), bf16[8,128,256]{2,1,0:T(8,128)(2,1)S(1)}, u32[]{:S(2)}, u32[]{:S(2)}) async-start(bf16[8,128,256]{2,1,0:T(8,128)(2,1)} %bitcast.200), calls=%async_computation.1 | async-start | bytes 1048576 | tf_op jit(solution)/shard_map/all_to_all | solution.py:37
  25.3 8.8 %all-to-all-done.1 = bf16[8,128,256]{2,1,0:T(8,128)(2,1)S(1)} async-done(((bf16[8,128,256]{2,1,0:T(8,128)(2,1)}), bf16[8,128,256]{2,1,0:T(8,128)(2,1)S(1)}, u32[]{:S(2)}, u32[]{:S(2)}) %all-to-all-start.1) | async-done | bytes 524320 | tf_op jit(solution)/shard_map/all_to_all | solution.py:37
  34.1 3.5 %all-to-all-start.2 = ((bf16[8,128,256]{2,1,0:T(8,128)(2,1)}), bf16[8,128,256]{2,1,0:T(8,128)(2,1)S(1)}, u32[]{:S(2)}, u32[]{:S(2)}) async-start(bf16[8,128,256]{2,1,0:T(8,128)(2,1)} %bitcast.198), calls=%async_computation.2 | async-start | bytes 1048576 | tf_op jit(solution)/shard_map/all_to_all | solution.py:37
  39.5 7.8 %all-to-all-done.2 = bf16[8,128,256]{2,1,0:T(8,128)(2,1)S(1)} async-done(((bf16[8,128,256]{2,1,0:T(8,128)(2,1)}), bf16[8,128,256]{2,1,0:T(8,128)(2,1)S(1)}, u32[]{:S(2)}, u32[]{:S(2)}) %all-to-all-start.2) | async-done | bytes 524320 | tf_op jit(solution)/shard_map/all_to_all | solution.py:37
  47.3 4.1 %all-to-all-start.4 = ((bf16[32,20,512]{2,1,0:T(8,128)(2,1)}), bf16[32,20,512]{2,1,0:T(8,128)(2,1)}, u32[]{:S(2)}, u32[]{:S(2)}) async-start(bf16[32,20,512]{2,1,0:T(8,128)(2,1)} %bitcast.20), calls=%async_computation.4 | async-start | bytes 1572864 | tf_op jit(solution)/shard_map/all_to_all | solution.py:37
  58.7 37.2 %all-to-all-done.4 = bf16[32,20,512]{2,1,0:T(8,128)(2,1)} async-done(((bf16[32,20,512]{2,1,0:T(8,128)(2,1)}), bf16[32,20,512]{2,1,0:T(8,128)(2,1)}, u32[]{:S(2)}, u32[]{:S(2)}) %all-to-all-start.4) | async-done | bytes 655392 | tf_op jit(solution)/shard_map/all_to_all | solution.py:37
  99.5 2.3 copy-done.2
  103.4 3.5 %fusion.15 = f32[2,512,2,128]{3,1,2,0:T(8,128)} fusion(pred[512,512]{1,0:T(8,128)(4,1)} %iota_compare_fusion.9, bf16[2,512,2,128]{3,2,1,0:T(2,128)(2,1)S(1)} %copy-done.4, bf16[2,512,2,128]{3,2,1,0:T(2,128)(2,1)} %copy-done.6, bf16[2,512,2,128]{3,2,1,0:T(2,128)(2,1)S(1)} %reshape_reshape.13), kind=kOutput, calls=%fused_computation.20 | convolution fusion | flops 538968064 | bytes 2883584 | tf_op jit(solution)/shard_map/nhts,nhtv->nhsv/dot_general | solution.py:172
  110.3 7.0 %collective-permute-start.3 = (bf16[160,2048]{1,0:T(8,128)(2,1)}, bf16[160,2048]{1,0:T(8,128)(2,1)}, u32[]{:S(2)}, u32[]{:S(2)}) collective-permute-start(bf16[160,2048]{1,0:T(8,128)(2,1)} %get-tuple-element.9), channel_id=1, source_target_pairs={{0,8},{8,0},{16,24},{24,16},{1,9},{9,1},{17,25},{25,17},{2,10},{10... | collective-permute-start | bytes 1966088 | tf_op jit(solution)/shard_map/ppermute | solution.py:42
  117.3 11.8 %collective-permute-done.4 = bf16[160,2048]{1,0:T(8,128)(2,1)} collective-permute-done((bf16[160,2048]{1,0:T(8,128)(2,1)}, bf16[160,2048]{1,0:T(8,128)(2,1)}, u32[]{:S(2)}, u32[]{:S(2)}) %collective-permute-start.4) | collective-permute-done | bytes 655392 | tf_op jit(solution)/shard_map/ppermute | solution.py:42
  129.1 2.6 fusion.22
  131.7 2.5 fusion.9
  134.3 4.2 %all-to-all-start.3 = ((bf16[8,160,256]{2,1,0:T(8,128)(2,1)}), bf16[8,160,256]{2,1,0:T(8,128)(2,1)}, u32[]{:S(2)}, u32[]{:S(2)}) async-start(bf16[8,160,256]{2,1,0:T(8,128)(2,1)} %bitcast.212), calls=%async_computation.3 | async-start | bytes 1310720 | tf_op jit(solution)/shard_map/all_to_all | solution.py:37
  138.5 11.2 %all-to-all-done.3 = bf16[8,160,256]{2,1,0:T(8,128)(2,1)} async-done(((bf16[8,160,256]{2,1,0:T(8,128)(2,1)}), bf16[8,160,256]{2,1,0:T(8,128)(2,1)}, u32[]{:S(2)}, u32[]{:S(2)}) %all-to-all-start.3) | async-done | bytes 655392 | tf_op jit(solution)/shard_map/all_to_all | solution.py:37
  151.6 11.8 %collective-permute-done.5 = bf16[160,2048]{1,0:T(8,128)(2,1)} collective-permute-done((bf16[160,2048]{1,0:T(8,128)(2,1)}, bf16[160,2048]{1,0:T(8,128)(2,1)}, u32[]{:S(2)}, u32[]{:S(2)}) %collective-permute-start.5) | collective-permute-done | bytes 655392 | tf_op jit(solution)/shard_map/ppermute | solution.py:42
  163.4 3.0 %fusion.23 = f32[160,2048]{1,0:T(8,128)} fusion(bf16[160,2048]{1,0:T(8,128)(2,1)} %collective-permute-done.5, bf16[160,2048]{1,0:T(8,128)(2,1)} %collective-permute-done.3, f32[4,160,2048]{2,1,0:T(8,128)} %bitcast.203, s32[]{:T(128)S(6)} %select_n.31), kind=kLoop, calls=%fused_computation.33 | loop fusion | flops 1310720 | bytes 3932164 | tf_op jit(solution)/shard_map/add | solution.py:57
  166.5 3.5 %fusion.10 = bf16[160,2048]{1,0:T(8,128)(2,1)S(1)} fusion(bf16[1,1024,2048]{2,1,0:T(8,128)(2,1)} %all-gather.3.cloned.1.call-done, f32[160,2048]{1,0:T(8,128)} %fusion.23), kind=kOutput, calls=%fused_computation.15 | convolution fusion | flops 672399360 | bytes 6160384 | tf_op jit(solution)/shard_map/dot_general | solution.py:21
  170.8 4.4 %all-to-all-start.6 = ((bf16[8,160,256]{2,1,0:T(8,128)(2,1)}), bf16[8,160,256]{2,1,0:T(8,128)(2,1)}, u32[]{:S(2)}, u32[]{:S(2)}) async-start(bf16[8,160,256]{2,1,0:T(8,128)(2,1)} %bitcast.204), calls=%async_computation.6 | async-start | bytes 1310720 | tf_op jit(solution)/shard_map/all_to_all | solution.py:37
  175.2 4.4 %multiply_convert_fusion.1 = (bf16[160,1024]{1,0:T(8,128)(2,1)S(1)}, bf16[160,1024]{1,0:T(8,128)(2,1)S(1)}) fusion(f32[160,2048]{1,0:T(8,128)} %fusion.23, bf16[160,2048]{1,0:T(8,128)(2,1)} %bitcast.211, bf16[1,1024,2048]{2,1,0:T(8,128)(2,1)} %all-gather.3.cloned.1.call-done), kind=kOutput, calls=%fused_computation.84 | convolution fusion | flops 673218560 | bytes 6815744 | tf_op jit(solution)/shard_map/dot_general | solution.py:25
  183.1 3.1 %all-to-all-done.6 = bf16[8,160,256]{2,1,0:T(8,128)(2,1)} async-done(((bf16[8,160,256]{2,1,0:T(8,128)(2,1)}), bf16[8,160,256]{2,1,0:T(8,128)(2,1)}, u32[]{:S(2)}, u32[]{:S(2)}) %all-to-all-start.6) | async-done | bytes 655392 | tf_op jit(solution)/shard_map/all_to_all | solution.py:37
  186.2 3.0 %fusion.27 = bf16[1024,256]{1,0:T(8,128)(2,1)} fusion(bf16[1280,256]{1,0:T(8,128)(2,1)} %bitcast.35, s32[1024]{0:T(1024)S(1)} %bitcast.219, f32[1024]{0:T(1024)S(1)} %bitcast.217), kind=kOutput, calls=%fused_computation.39 | convolution fusion | flops 672923648 | bytes 1187840 | tf_op jit(solution)/shard_map/dot_general | solution.py:21
  193.6 3.2 %collective-permute-start.11 = (f32[2,128,128]{1,2,0:T(8,128)S(1)}, f32[2,128,128]{1,2,0:T(8,128)S(1)}, u32[]{:S(2)}, u32[]{:S(2)}) collective-permute-start(f32[2,128,128]{1,2,0:T(8,128)S(1)} %get-tuple-element.17), channel_id=1, source_target_pairs={{0,24},{1,25},{2,26},{3,27},{4,28},{5,29},{6,30},{7,31}} | collective-permute-start | bytes 393224 | tf_op jit(solution)/shard_map/ppermute | solution.py:209
  198.8 3.1 %collective-permute-start.9 = (f32[2,128,128]{1,2,0:T(8,128)S(1)}, f32[2,128,128]{1,2,0:T(8,128)}, u32[]{:S(2)}, u32[]{:S(2)}) collective-permute-start(f32[2,128,128]{1,2,0:T(8,128)S(1)} %get-tuple-element.17), channel_id=1, source_target_pairs={{0,8},{8,16},{16,24},{1,9},{9,17},{17,25},{2,10},{10,18},{18,26},{... | collective-permute-start | bytes 393224 | tf_op jit(solution)/shard_map/ppermute | solution.py:209
  206.6 3.9 %all-to-all-start.8 = ((bf16[8,128,256]{2,1,0:T(8,128)(2,1)}), bf16[8,128,256]{2,1,0:T(8,128)(2,1)S(1)}, u32[]{:S(2)}, u32[]{:S(2)}) async-start(bf16[8,128,256]{2,1,0:T(8,128)(2,1)} %reshape_reshape.15), calls=%async_computation.8 | async-start | bytes 1048576 | tf_op jit(solution)/shard_map/all_to_all | solution.py:37
  212.1 2.1 fusion.38
  221.3 3.9 %all-to-all-start.7 = ((bf16[8,128,256]{2,1,0:T(8,128)(2,1)}), bf16[8,128,256]{2,1,0:T(8,128)(2,1)S(1)}, u32[]{:S(2)}, u32[]{:S(2)}) async-start(bf16[8,128,256]{2,1,0:T(8,128)(2,1)} %reshape_reshape.14), calls=%async_computation.7 | async-start | bytes 1048576 | tf_op jit(solution)/shard_map/all_to_all | solution.py:37
  225.2 6.8 %collective-permute-done.8 = bf16[160,2048]{1,0:T(8,128)(2,1)} collective-permute-done((bf16[160,2048]{1,0:T(8,128)(2,1)}, bf16[160,2048]{1,0:T(8,128)(2,1)}, u32[]{:S(2)}, u32[]{:S(2)}) %collective-permute-start.8) | collective-permute-done | bytes 655392 | tf_op jit(solution)/shard_map/ppermute | solution.py:42
  233.6 2.1 fusion.34
  237.7 4.9 %all-to-all-start.5 = ((bf16[32,20,512]{2,1,0:T(8,128)(2,1)}), bf16[32,20,512]{2,1,0:T(8,128)(2,1)S(1)}, u32[]{:S(2)}, u32[]{:S(2)}) async-start(bf16[32,20,512]{2,1,0:T(8,128)(2,1)} %reshape.134), calls=%async_computation.5 | async-start | bytes 1572864 | tf_op jit(solution)/shard_map/all_to_all | solution.py:37
  247.0 16.3 %all-to-all-done.5 = bf16[32,20,512]{2,1,0:T(8,128)(2,1)S(1)} async-done(((bf16[32,20,512]{2,1,0:T(8,128)(2,1)}), bf16[32,20,512]{2,1,0:T(8,128)(2,1)S(1)}, u32[]{:S(2)}, u32[]{:S(2)}) %all-to-all-start.5) | async-done | bytes 655392 | tf_op jit(solution)/shard_map/all_to_all | solution.py:37
  (114 shorter events, 59.2 us)
Async XLA Ops:
  7.2 90.8 %copy-start = (bf16[1,512,1024]{2,1,0:T(8,128)(2,1)S(1)}, bf16[1,512,1024]{2,1,0:T(8,128)(2,1)}, u32[]{:S(2)}) copy-start(bf16[1,512,1024]{2,1,0:T(8,128)(2,1)} %param.12) | copy-start | bytes 3145732
  7.2 17.3 %copy-start.12 = (bf16[128,2048]{1,0:T(8,128)(2,1)S(1)}, bf16[128,2048]{1,0:T(8,128)(2,1)}, u32[]{:S(2)}) copy-start(bf16[128,2048]{1,0:T(8,128)(2,1)} %param.16) | copy-start | bytes 1572868
  7.2 159.3 %all-gather.3.cloned.1.call-start = ((), (), s32[]{:S(2)}) async-start(), calls=%async_computation.9 | async-start | bytes 5242880 | tf_op jit(solution)/shard_map/all_gather | solution.py:100
  10.9 10.0 %all-to-all-start = ((f32[8,8,128]{2,1,0:T(8,128)}), f32[8,8,128]{2,1,0:T(8,128)S(1)}, u32[]{:S(2)}, u32[]{:S(2)}) async-start(f32[8,8,128]{2,1,0:T(8,128)} %broadcast_in_dim.61), calls=%async_computation | async-start | bytes 65536 | tf_op jit(solution)/shard_map/all_to_all | solution.py:37
  16.1 21.5 %copy-start.17 = (s32[128,1]{0,1:T(1,128)S(1)}, s32[128,1]{0,1:T(1,128)}, u32[]{:S(2)}) copy-start(s32[128,1]{0,1:T(1,128)} %param.10) | copy-start | bytes 1540
  16.1 21.6 %copy-start.13 = (bf16[128,2048]{1,0:T(8,128)(2,1)S(1)}, bf16[128,2048]{1,0:T(8,128)(2,1)}, u32[]{:S(2)}) copy-start(bf16[128,2048]{1,0:T(8,128)(2,1)} %param.9) | copy-start | bytes 1572868
  20.9 13.2 %all-to-all-start.1 = ((bf16[8,128,256]{2,1,0:T(8,128)(2,1)}), bf16[8,128,256]{2,1,0:T(8,128)(2,1)S(1)}, u32[]{:S(2)}, u32[]{:S(2)}) async-start(bf16[8,128,256]{2,1,0:T(8,128)(2,1)} %bitcast.200), calls=%async_computation.1 | async-start | bytes 1048576 | tf_op jit(solution)/shard_map/all_to_all | solution.py:37
  34.1 13.2 %all-to-all-start.2 = ((bf16[8,128,256]{2,1,0:T(8,128)(2,1)}), bf16[8,128,256]{2,1,0:T(8,128)(2,1)S(1)}, u32[]{:S(2)}, u32[]{:S(2)}) async-start(bf16[8,128,256]{2,1,0:T(8,128)(2,1)} %bitcast.198), calls=%async_computation.2 | async-start | bytes 1048576 | tf_op jit(solution)/shard_map/all_to_all | solution.py:37
  38.0 13.4 %copy-start.14 = (bf16[1024,256]{1,0:T(8,128)(2,1)S(1)}, bf16[1024,256]{1,0:T(8,128)(2,1)}, u32[]{:S(2)}) copy-start(bf16[1024,256]{1,0:T(8,128)(2,1)} %param.17) | copy-start | bytes 1572868
  39.5 12.9 %copy-start.11 = (bf16[8,128,256]{2,1,0:T(8,128)(2,1)S(1)}, bf16[8,128,256]{2,1,0:T(8,128)(2,1)}, u32[]{:S(2)}) copy-start(bf16[8,128,256]{2,1,0:T(8,128)(2,1)} %copy-done.10) | copy-start | bytes 1572868
  47.3 48.6 %all-to-all-start.4 = ((bf16[32,20,512]{2,1,0:T(8,128)(2,1)}), bf16[32,20,512]{2,1,0:T(8,128)(2,1)}, u32[]{:S(2)}, u32[]{:S(2)}) async-start(bf16[32,20,512]{2,1,0:T(8,128)(2,1)} %bitcast.20), calls=%async_computation.4 | async-start | bytes 1572864 | tf_op jit(solution)/shard_map/all_to_all | solution.py:37
  52.6 6.1 %copy-start.3 = (bf16[2,512,2,128]{3,2,1,0:T(2,128)(2,1)}, bf16[2,512,2,128]{3,2,1,0:T(2,128)(2,1)S(1)}, u32[]{:S(2)}) copy-start(bf16[2,512,2,128]{3,2,1,0:T(2,128)(2,1)S(1)} %reshape_reshape.12) | copy-start | bytes 1572868
  52.6 44.5 %copy-start.1 = (bf16[1,512,1024]{2,1,0:T(8,128)(2,1)S(1)}, bf16[1,512,1024]{2,1,0:T(8,128)(2,1)}, u32[]{:S(2)}) copy-start(bf16[1,512,1024]{2,1,0:T(8,128)(2,1)} %param.13) | copy-start | bytes 3145732
  53.6 53.3 %collective-permute-start.2 = (f32[2,128,128]{2,1,0:T(8,128)}, f32[2,128,128]{2,1,0:T(8,128)}, u32[]{:S(2)}, u32[]{:S(2)}) collective-permute-start(f32[2,128,128]{2,1,0:T(8,128)} %get-tuple-element.15), channel_id=1, source_target_pairs={{24,0},{25,1},{26,2},{27,3},{28,4},{29,5},{30,6},{31,7}} | collective-permute-start | bytes 393224 | tf_op jit(solution)/shard_map/ppermute | solution.py:160
  54.9 52.1 %collective-permute-start.1 = (f32[2,128,128]{2,1,0:T(8,128)}, f32[2,128,128]{2,1,0:T(8,128)}, u32[]{:S(2)}, u32[]{:S(2)}) collective-permute-start(f32[2,128,128]{2,1,0:T(8,128)} %get-tuple-element.15), channel_id=1, source_target_pairs={{16,0},{24,8},{17,1},{25,9},{18,2},{26,10},{19,3},{27,11},{20,4},{... | collective-permute-start | bytes 393224 | tf_op jit(solution)/shard_map/ppermute | solution.py:160
  56.2 50.8 %collective-permute-start = (f32[2,128,128]{2,1,0:T(8,128)}, f32[2,128,128]{2,1,0:T(8,128)}, u32[]{:S(2)}, u32[]{:S(2)}) collective-permute-start(f32[2,128,128]{2,1,0:T(8,128)} %get-tuple-element.15), channel_id=1, source_target_pairs={{8,0},{16,8},{24,16},{9,1},{17,9},{25,17},{10,2},{18,10},{26,18},{... | collective-permute-start | bytes 393224 | tf_op jit(solution)/shard_map/ppermute | solution.py:160
  103.1 26.1 %collective-permute-start.4 = (bf16[160,2048]{1,0:T(8,128)(2,1)}, bf16[160,2048]{1,0:T(8,128)(2,1)}, u32[]{:S(2)}, u32[]{:S(2)}) collective-permute-start(bf16[160,2048]{1,0:T(8,128)(2,1)} %get-tuple-element.10), channel_id=1, source_target_pairs={{0,8},{8,0},{16,24},{24,16},{1,9},{9,1},{17,25},{25,17},{2,10},{10... | collective-permute-start | bytes 1966088 | tf_op jit(solution)/shard_map/ppermute | solution.py:42
  110.3 41.4 %collective-permute-start.3 = (bf16[160,2048]{1,0:T(8,128)(2,1)}, bf16[160,2048]{1,0:T(8,128)(2,1)}, u32[]{:S(2)}, u32[]{:S(2)}) collective-permute-start(bf16[160,2048]{1,0:T(8,128)(2,1)} %get-tuple-element.9), channel_id=1, source_target_pairs={{0,8},{8,0},{16,24},{24,16},{1,9},{9,1},{17,25},{25,17},{2,10},{10... | collective-permute-start | bytes 1966088 | tf_op jit(solution)/shard_map/ppermute | solution.py:42
  131.7 31.7 %collective-permute-start.5 = (bf16[160,2048]{1,0:T(8,128)(2,1)}, bf16[160,2048]{1,0:T(8,128)(2,1)}, u32[]{:S(2)}, u32[]{:S(2)}) collective-permute-start(bf16[160,2048]{1,0:T(8,128)(2,1)} %fusion.22), channel_id=1, source_target_pairs={{0,16},{8,24},{16,0},{24,8},{1,17},{9,25},{17,1},{25,9},{2,18},{10... | collective-permute-start | bytes 1966088 | tf_op jit(solution)/shard_map/ppermute | solution.py:42
  134.3 15.4 %all-to-all-start.3 = ((bf16[8,160,256]{2,1,0:T(8,128)(2,1)}), bf16[8,160,256]{2,1,0:T(8,128)(2,1)}, u32[]{:S(2)}, u32[]{:S(2)}) async-start(bf16[8,160,256]{2,1,0:T(8,128)(2,1)} %bitcast.212), calls=%async_computation.3 | async-start | bytes 1310720 | tf_op jit(solution)/shard_map/all_to_all | solution.py:37
  170.8 15.4 %all-to-all-start.6 = ((bf16[8,160,256]{2,1,0:T(8,128)(2,1)}), bf16[8,160,256]{2,1,0:T(8,128)(2,1)}, u32[]{:S(2)}, u32[]{:S(2)}) async-start(bf16[8,160,256]{2,1,0:T(8,128)(2,1)} %bitcast.204), calls=%async_computation.6 | async-start | bytes 1310720 | tf_op jit(solution)/shard_map/all_to_all | solution.py:37
  180.5 30.0 %collective-permute-start.6 = (bf16[160,2048]{1,0:T(8,128)(2,1)}, bf16[160,2048]{1,0:T(8,128)(2,1)}, u32[]{:S(2)}, u32[]{:S(2)}) collective-permute-start(bf16[160,2048]{1,0:T(8,128)(2,1)} %pad_maximum_fusion.1), channel_id=1, source_target_pairs={{0,16},{8,24},{16,0},{24,8},{1,17},{9,25},{17,1},{25,9},{2,18},{10... | collective-permute-start | bytes 1966088 | tf_op jit(solution)/shard_map/ppermute | solution.py:42
  180.5 33.7 %collective-permute-start.7 = (bf16[160,2048]{1,0:T(8,128)(2,1)}, bf16[160,2048]{1,0:T(8,128)(2,1)}, u32[]{:S(2)}, u32[]{:S(2)}) collective-permute-start(bf16[160,2048]{1,0:T(8,128)(2,1)} %pad_maximum_fusion.1), channel_id=1, source_target_pairs={{0,8},{8,0},{16,24},{24,16},{1,9},{9,1},{17,25},{25,17},{2,10},{10... | collective-permute-start | bytes 1966088 | tf_op jit(solution)/shard_map/ppermute | solution.py:42
  186.2 5.0 %copy-start.15 = (pred[512,512]{1,0:T(8,128)(4,1)S(1)}, pred[512,512]{1,0:T(8,128)(4,1)}, u32[]{:S(2)}) copy-start(pred[512,512]{1,0:T(8,128)(4,1)} %iota_compare_fusion.9) | copy-start | bytes 786436
  193.6 24.3 %collective-permute-start.11 = (f32[2,128,128]{1,2,0:T(8,128)S(1)}, f32[2,128,128]{1,2,0:T(8,128)S(1)}, u32[]{:S(2)}, u32[]{:S(2)}) collective-permute-start(f32[2,128,128]{1,2,0:T(8,128)S(1)} %get-tuple-element.17), channel_id=1, source_target_pairs={{0,24},{1,25},{2,26},{3,27},{4,28},{5,29},{6,30},{7,31}} | collective-permute-start | bytes 393224 | tf_op jit(solution)/shard_map/ppermute | solution.py:209
  196.8 21.2 %collective-permute-start.10 = (f32[2,128,128]{1,2,0:T(8,128)S(1)}, f32[2,128,128]{1,2,0:T(8,128)}, u32[]{:S(2)}, u32[]{:S(2)}) collective-permute-start(f32[2,128,128]{1,2,0:T(8,128)S(1)} %get-tuple-element.17), channel_id=1, source_target_pairs={{0,16},{8,24},{1,17},{9,25},{2,18},{10,26},{3,19},{11,27},{4,20},{... | collective-permute-start | bytes 393224 | tf_op jit(solution)/shard_map/ppermute | solution.py:209
  198.8 19.6 %collective-permute-start.9 = (f32[2,128,128]{1,2,0:T(8,128)S(1)}, f32[2,128,128]{1,2,0:T(8,128)}, u32[]{:S(2)}, u32[]{:S(2)}) collective-permute-start(f32[2,128,128]{1,2,0:T(8,128)S(1)} %get-tuple-element.17), channel_id=1, source_target_pairs={{0,8},{8,16},{16,24},{1,9},{9,17},{17,25},{2,10},{10,18},{18,26},{... | collective-permute-start | bytes 393224 | tf_op jit(solution)/shard_map/ppermute | solution.py:209
  206.6 14.7 %all-to-all-start.8 = ((bf16[8,128,256]{2,1,0:T(8,128)(2,1)}), bf16[8,128,256]{2,1,0:T(8,128)(2,1)S(1)}, u32[]{:S(2)}, u32[]{:S(2)}) async-start(bf16[8,128,256]{2,1,0:T(8,128)(2,1)} %reshape_reshape.15), calls=%async_computation.8 | async-start | bytes 1048576 | tf_op jit(solution)/shard_map/all_to_all | solution.py:37
  210.5 21.6 %collective-permute-start.8 = (bf16[160,2048]{1,0:T(8,128)(2,1)}, bf16[160,2048]{1,0:T(8,128)(2,1)}, u32[]{:S(2)}, u32[]{:S(2)}) collective-permute-start(bf16[160,2048]{1,0:T(8,128)(2,1)} %collective-permute-done.6), channel_id=1, source_target_pairs={{0,8},{8,0},{16,24},{24,16},{1,9},{9,1},{17,25},{25,17},{2,10},{10... | collective-permute-start | bytes 1966088 | tf_op jit(solution)/shard_map/ppermute | solution.py:42
  221.3 16.4 %all-to-all-start.7 = ((bf16[8,128,256]{2,1,0:T(8,128)(2,1)}), bf16[8,128,256]{2,1,0:T(8,128)(2,1)S(1)}, u32[]{:S(2)}, u32[]{:S(2)}) async-start(bf16[8,128,256]{2,1,0:T(8,128)(2,1)} %reshape_reshape.14), calls=%async_computation.7 | async-start | bytes 1048576 | tf_op jit(solution)/shard_map/all_to_all | solution.py:37
  237.7 25.5 %all-to-all-start.5 = ((bf16[32,20,512]{2,1,0:T(8,128)(2,1)}), bf16[32,20,512]{2,1,0:T(8,128)(2,1)S(1)}, u32[]{:S(2)}, u32[]{:S(2)}) async-start(bf16[32,20,512]{2,1,0:T(8,128)(2,1)} %reshape.134), calls=%async_computation.5 | async-start | bytes 1572864 | tf_op jit(solution)/shard_map/all_to_all | solution.py:37
  246.0 17.5 %copy-start.16 = (f32[128,1]{0,1:T(1,128)S(1)}, f32[128,1]{0,1:T(1,128)}, u32[]{:S(2)}) copy-start(f32[128,1]{0,1:T(1,128)} %param.11) | copy-start | bytes 1540
  (8 other events, 28.9 us)
Sparse Core Ops, SparseCore 0:
  9.6 111.3 all-gather.2

commit v2 on v1

v2 whole, which is shorter than its diff:
```python
import functools
import math

import jax
import jax.numpy as jnp
from jax import lax
from jax.experimental import pallas as pl
from jax.experimental.pallas import tpu as pltpu
from jax.sharding import Mesh
from jax.sharding import PartitionSpec as P

HEAD_DIM = 128
TOPK = 1
BLOCK = 512
VMEM_LIMIT = 32 * 1024 * 1024
BF16 = jnp.bfloat16
F32 = jnp.float32


def dot(left, right):
    return jnp.dot(left, right, preferred_element_type=F32)


def dot_nt(left, right):
    return lax.dot_general(left, right, (((1,), (1,)), ((), ())), preferred_element_type=F32)


def dot_tn(left, right):
    return lax.dot_general(left, right, (((0,), (0,)), ((), ())), preferred_element_type=F32)


def iota(shape, axis):
    return lax.broadcasted_iota(jnp.int32, shape, axis)


def run(kernel, outs, args, scratch=(), us=1):
    in_specs = [
        pl.BlockSpec(memory_space=pltpu.SMEM if a.dtype == jnp.int32 and a.ndim == 1 else pltpu.VMEM)
        for a in args
    ]
    moved = sum(math.prod(a.shape) * a.dtype.itemsize for a in (*args, *outs))
    return pl.pallas_call(
        kernel,
        out_shape=tuple(outs),
        in_specs=in_specs,
        out_specs=tuple(pl.BlockSpec(memory_space=pltpu.VMEM) for _ in outs),
        scratch_shapes=list(scratch),
        compiler_params=pltpu.CompilerParams(vmem_limit_bytes=VMEM_LIMIT),
        cost_estimate=pl.CostEstimate(flops=int(us * 1.15e9), bytes_accessed=moved // 100, transcendentals=0),
    )(*args)


def shape(dims, dtype):
    return jax.ShapeDtypeStruct(dims, dtype)


def row_slots(ids, pad, wide):
    rows = ids.shape[0]
    named = ids == iota((rows, 128 * -(-wide // 128)), 1)
    earlier = (iota((rows, rows), 1) < iota((rows, rows), 0)).astype(BF16)
    counts = dot(earlier, named.astype(BF16))
    rank = jnp.sum(jnp.where(named, counts, 0.0), axis=1, keepdims=True).astype(jnp.int32)
    chosen = (ids * pad + rank == iota((rows, wide * pad), 1)).astype(BF16)
    return rank, chosen


def packing(experts, capacity, pad):
    slots = experts * capacity
    row, col = iota((slots, experts * pad), 0), iota((slots, experts * pad), 1)
    expert = col // pad
    inner = col - expert * pad
    return ((inner < capacity) & (row == expert * capacity + inner)).astype(BF16)


def unpacking(experts, capacity, pad):
    slots = experts * capacity
    row, col = iota((experts * pad, slots), 0), iota((experts * pad, slots), 1)
    expert = row // pad
    inner = row - expert * pad
    return ((inner < capacity) & (col == expert * capacity + inner)).astype(BF16)


FACTS = 16


def route_kernel(
    hi, exp, group, capacity, pad, ids_ref, gate_ref, tokens_ref, query_ref, key_ref, out_ref, query_out, key_out
):
    rows, width = tokens_ref.shape
    part = width // hi
    ids = ids_ref[...]
    rank, chosen = row_slots(ids, pad, exp)
    slot_rows = dot_tn(chosen, tokens_ref[...]).astype(BF16)
    for c in range(hi):
        for e in range(exp):
            out_ref[c * exp + e] = slot_rows[e * pad : e * pad + capacity, c * part : (c + 1) * part]
    gate = gate_ref[...]
    high = gate.astype(BF16).astype(F32)
    mid = (gate - high).astype(BF16).astype(F32)
    lane = iota((rows, 128), 1)
    facts = jnp.zeros((rows, 128), F32)
    for col, fact in enumerate((ids.astype(F32), rank.astype(F32), high, mid, gate - high - mid)):
        facts = jnp.where(lane == col, fact, facts)
    facts = facts.T[:FACTS].astype(BF16)
    key_width = key_out.shape[2]
    for e in range(exp):
        cols = slice(e // group * key_width, (e // group + 1) * key_width)
        query_out[e] = query_ref[:, cols]
        key_out[e, :rows] = key_ref[:, cols]
        key_out[e, rows:] = jnp.zeros((FACTS, key_width), BF16)
        key_out[e, rows:, :rows] = facts


def facts_of(key_ref, source):
    rows = key_ref.shape[1] - FACTS
    return key_ref[source, rows:, :rows].astype(F32)


def key_rows(key_ref, block, cols):
    rows = key_ref.shape[1] - FACTS
    each = BLOCK // rows
    return jnp.concatenate([key_ref[s, :rows, cols] for s in range(block * each, (block + 1) * each)], axis=0)


def slice_cols(index, width):
    return pl.ds(pl.multiple_of(index * width, 128), width)


def project_kernel(ctx, exp, capacity, pad, me_ref, in_ref, gate_ref, up_ref, *rest):
    out_refs, (padded, packed) = rest[:-2], rest[-2:]
    slots = exp * capacity
    hidden = gate_ref.shape[1]
    select = packing(exp, capacity, pad)
    padded[...] = jnp.zeros_like(padded)
    for offset in range(ctx):
        chunk = me_ref[0] ^ offset
        for e in range(exp):
            padded[e * pad : e * pad + capacity, :] = in_ref[chunk * exp + e]
        packed[offset * slots : (offset + 1) * slots, :] = dot(select, padded[...]).astype(BF16)
    for col, weight in enumerate((gate_ref, up_ref)):
        product = dot(packed[...], weight[...])
        for offset in range(ctx):
            out_refs[offset][:, col * hidden : (col + 1) * hidden] = product[
                offset * slots : (offset + 1) * slots
            ].astype(out_refs[offset].dtype)


def gates_kernel(terms, me_ref, grads_ref, *rest):
    sums, downs, (out_ref, active_ref, rows) = rest[:terms], rest[terms:-3], rest[-3:]
    hidden, depth = downs[0].shape
    parts, _, part = grads_ref.shape
    for e in range(parts):
        rows[:, e * part : (e + 1) * part] = grads_ref[e]
    projected = sums[0][...]
    for other in sums[1:]:
        projected = projected + other[...].astype(F32)
    gate, up = projected[:, :hidden], projected[:, hidden:]
    sigmoid = jax.nn.sigmoid(gate)
    active = gate * sigmoid
    active_ref[...] = (active * up).astype(BF16)
    grad = 0.0
    for o, down in enumerate(downs):
        grad += dot_nt(rows[:, slice_cols(me_ref[0] ^ o if len(downs) > 1 else 0, depth)], down[...])
    out_ref[:, :hidden] = (grad * up * (sigmoid * (1.0 + gate * (1.0 - sigmoid)))).astype(BF16)
    out_ref[:, hidden:] = (grad * active).astype(BF16)


def forward_kernel(me_ref, active_ref, *rest):
    downs, out_ref = rest[:-1], rest[-1]
    parts, _, part = out_ref.shape
    each = parts // len(downs)
    for o, down in enumerate(downs):
        product = dot(active_ref[...], down[...]).astype(BF16)
        for b in range(each):
            place = (me_ref[0] ^ o) * each + b if len(downs) > 1 else b
            out_ref[place] = product[:, b * part : (b + 1) * part]


def backward_kernel(ctx, exp, capacity, pad, me_ref, gate_ref, up_ref, *rest):
    chunks, (out_ref, grads) = rest[:-2], rest[-2:]
    hidden = gate_ref.shape[1]
    slots = exp * capacity
    for offset in range(ctx):
        grads[offset * slots : (offset + 1) * slots, :] = chunks[offset][...]
    product = (dot_nt(grads[:, :hidden], gate_ref[...]) + dot_nt(grads[:, hidden:], up_ref[...])).astype(BF16)
    spread = unpacking(exp, capacity, pad)
    for offset in range(ctx):
        chunk = me_ref[0] ^ offset
        rows = dot(spread, product[offset * slots : (offset + 1) * slots]).astype(BF16)
        for e in range(exp):
            out_ref[chunk * exp + e] = rows[e * pad : e * pad + capacity]


def home_kernel(ctx, exp, capacity, pad, ids_ref, gate_ref, in_ref, out_ref, padded):
    part = in_ref.shape[2]
    rank, chosen = row_slots(ids_ref[...], pad, exp)
    padded[...] = jnp.zeros_like(padded)
    for c in range(ctx):
        for e in range(exp):
            padded[e * pad : e * pad + capacity, c * part : (c + 1) * part] = in_ref[c * exp + e]
    out_ref[...] = (gate_ref[...] * dot(chosen, padded[...])).astype(BF16)


def row_place(ids, rank, source, capacity, slots):
    return ids * slots + source * capacity + rank


def after_kernel(heads, query_ref, cot_ref, out_ref):
    width = cot_ref.shape[1] // heads
    for h in range(heads):
        out_ref[h] = dot_tn(
            query_ref[:, h * HEAD_DIM : (h + 1) * HEAD_DIM], cot_ref[:, h * width : (h + 1) * width]
        ).astype(BF16)


def grad_values_kernel(heads, capacity, scale, query_ref, key_ref, cot_ref, *rest):
    arrived, (out_ref, low_ref, grads) = rest[:-3], rest[-3:]
    span, total = cot_ref.shape
    width = total // heads
    blocks = span // BLOCK
    causal = iota((BLOCK, BLOCK), 0) >= iota((BLOCK, BLOCK), 1)
    for h in range(heads):
        keys, cols = slice(h * HEAD_DIM, (h + 1) * HEAD_DIM), slice(h * width, (h + 1) * width)
        state = arrived[0][h].astype(F32)
        for other in arrived[1:]:
            state = state + other[h].astype(F32)
        for n in reversed(range(blocks)):
            rows = slice(n * BLOCK, (n + 1) * BLOCK)
            low = state.astype(BF16)
            low_ref[n * heads + h] = low
            query, key, cot = query_ref[rows, keys], key_rows(key_ref, n, keys), cot_ref[rows, cols]
            scores = jnp.where(causal, dot_nt(query, key), 0.0).astype(BF16)
            grads[rows, cols] = (scale * (dot_tn(scores, cot) + dot(key, low))).astype(BF16)
            if n:
                state = state + dot_tn(query, cot)
    sources, slots = key_ref.shape[0], out_ref.shape[1]
    facts = [facts_of(key_ref, s) for s in range(sources)]
    place = jnp.concatenate(
        [
            row_place(
                facts[s][0:1].astype(jnp.int32), facts[s][1:2].astype(jnp.int32), s, capacity, slots
            )
            for s in range(sources)
        ],
        axis=1,
    )
    row = iota((slots, span), 0)
    for e in range(out_ref.shape[0]):
        chosen = (place == row + e * slots).astype(BF16)
        out_ref[e] = dot(chosen, grads[...]).astype(BF16)


def grad_heads_kernel(
    heads, capacity, scale, query_ref, key_ref, cot_ref, low_ref, in_ref, key_out, part_out, state_out
):
    span, total = cot_ref.shape
    width = total // heads
    blocks = span // BLOCK
    slots = in_ref.shape[1]
    rows_each = key_ref.shape[1] - FACTS
    returned = in_ref[...].reshape(-1, total)
    causal = iota((BLOCK, BLOCK), 0) >= iota((BLOCK, BLOCK), 1)
    states = [jnp.zeros((HEAD_DIM, width), F32) for _ in range(heads)]
    for n in range(blocks):
        rows = slice(n * BLOCK, (n + 1) * BLOCK)
        places, weights = [], []
        for s in range(n * BLOCK // rows_each, (n + 1) * BLOCK // rows_each):
            facts = facts_of(key_ref, s).T
            places.append(
                row_place(
                    facts[:, 0:1].astype(jnp.int32), facts[:, 1:2].astype(jnp.int32), s, capacity, slots
                )
            )
            weights.append(facts[:, 2:3] + facts[:, 3:4] + facts[:, 4:5])
        place, weight = jnp.concatenate(places, axis=0), jnp.concatenate(weights, axis=0)
        chosen = (place == iota((BLOCK, returned.shape[0]), 1)).astype(BF16)
        values = (weight * dot(chosen, returned)).astype(BF16)
        for h in range(heads):
            keys, cols = slice(h * HEAD_DIM, (h + 1) * HEAD_DIM), slice(h * width, (h + 1) * width)
            query, key, cot = query_ref[rows, keys], key_rows(key_ref, n, keys), cot_ref[rows, cols]
            value = values[:, cols]
            probes = jnp.where(causal, dot_nt(cot, value), 0.0).astype(BF16)
            key_out[rows, keys] = (
                scale * (dot_tn(probes, query) + dot_nt(value, low_ref[n * heads + h]))
            ).astype(BF16)
            part = dot(probes, key)
            if n:
                part = part + dot_nt(cot, states[h].astype(BF16))
            part_out[rows, keys] = part
            states[h] = states[h] + dot_tn(key, value)
    for h in range(heads):
        state_out[h] = states[h].astype(BF16)


def finish_kernel(heads, scale, cot_ref, part_ref, grad_key_ref, *rest):
    arrived, out_ref = rest[:-1], rest[-1]
    width = cot_ref.shape[1] // heads
    sources, rows = out_ref.shape[0] // 2, out_ref.shape[1]
    for h in range(heads):
        keys, cols = slice(h * HEAD_DIM, (h + 1) * HEAD_DIM), slice(h * width, (h + 1) * width)
        state = arrived[0][h].astype(F32)
        for other in arrived[1:]:
            state = state + other[h].astype(F32)
        grad = (scale * (part_ref[:, keys] + dot_nt(cot_ref[:, cols], state.astype(BF16)))).astype(BF16)
        for s in range(sources):
            out_ref[2 * s, :, keys] = grad[s * rows : (s + 1) * rows]
    for s in range(sources):
        out_ref[2 * s + 1] = grad_key_ref[s * rows : (s + 1) * rows]


def heads_kernel(group, in_ref, query_ref, key_ref):
    sources, both, key_width = in_ref.shape
    rows = both // 2
    for n in range(sources // group):
        for place, out in enumerate((query_ref, key_ref)):
            inner = slice(place * rows, (place + 1) * rows)
            total = in_ref[n * group, inner]
            if group > 1:
                total = total.astype(F32)
                for part in range(1, group):
                    total = total + in_ref[n * group + part, inner].astype(F32)
            out[:, n * key_width : (n + 1) * key_width] = total.astype(BF16)


def move(buffer, axes):
    return lax.all_to_all(buffer, axes, split_axis=0, concat_axis=0, tiled=True)


CTX = ("hi", "lo")
ALL = ("hi", "lo", "exp")


def swap(block, distance):
    count = lax.axis_size("hi") * lax.axis_size("lo")
    return lax.ppermute(block, CTX, [(i, i ^ distance) for i in range(count)])


def spread_rest(chunks, distances):
    chunks = dict(chunks)
    for distance in sorted(distances, reverse=True):
        for o in [o for o in chunks if not o & distance and o and o | distance not in chunks and o > distance]:
            chunks[o | distance] = swap(chunks[o], distance)
    return chunks


def sum_own(terms):
    count, distance = len(terms), 1
    held, own = dict(enumerate(terms)), [terms[0]]
    while distance < count:
        urgent = sorted((o for o in held if o & distance and o != distance), reverse=True)
        arrived = {o ^ distance: swap(held[o].astype(BF16), distance) for o in urgent}
        last = held[distance].astype(BF16)
        held = {o: held[o].astype(F32) + term.astype(F32) for o, term in arrived.items()}
        if held:
            first = max(held)
            held[first] = held[first].astype(BF16)
        own.append(swap(last, distance))
        distance *= 2
    return own


def shards(
    tokens,
    expert_ids,
    gate_weights,
    weight_gate,
    weight_up,
    weight_down,
    attn_queries,
    attn_keys,
    grad_out,
):
    exp, hi, lo = lax.axis_size("exp"), lax.axis_size("hi"), lax.axis_size("lo")
    ctx = hi * lo
    rows, width = tokens.shape
    slice_width, hidden = weight_gate.shape[1:]
    capacity = 5 * rows * TOPK // (4 * exp)
    pad = 16 * -(-capacity // 16)
    slots = exp * capacity
    part_width = width // exp
    key_width = max(part_width, HEAD_DIM)
    group = key_width // part_width
    heads = key_width // HEAD_DIM
    span = rows * exp
    scale = 1.0 / math.sqrt(HEAD_DIM * span * ctx)
    me = lax.axis_index(CTX).astype(jnp.int32).reshape(1)
    state_low = shape((heads, HEAD_DIM, part_width // heads), BF16)

    outgoing, query, key = run(
        functools.partial(route_kernel, ctx, exp, group, capacity, pad),
        [
            shape((ctx * exp, capacity, slice_width), BF16),
            shape((exp, rows, key_width), BF16),
            shape((exp, rows + FACTS, key_width), BF16),
        ],
        [expert_ids, gate_weights, tokens, attn_queries, attn_keys],
    )
    doubling = [1 << n for n in range((ctx - 1).bit_length())]

    downs = {0: weight_down[0]}
    for distance in reversed(doubling):
        downs[distance] = swap(weight_down[0], distance)

    straight = [downs[d] for d in doubling]

    query = move(query, "exp").reshape(span, key_width)
    key, query = lax.optimization_barrier((key, query))
    (after,) = run(functools.partial(after_kernel, heads), [state_low], [query, grad_out])
    after_in = [
        lax.ppermute(after, CTX, [(i + step, i) for i in range(ctx - step)]) for step in range(1, ctx)
    ]
    key = move(key, "exp")
    outgoing, key, straight = lax.optimization_barrier((outgoing, key, straight))
    incoming = move(outgoing, ALL)
    downs = spread_rest({0: downs[0], **dict(zip(doubling, straight, strict=True))}, doubling)
    rest = [downs[o] for o in range(1, ctx) if o & (o - 1)]

    terms = run(
        functools.partial(project_kernel, ctx, exp, capacity, pad),
        [shape((slots, 2 * hidden), BF16 if o & 1 else F32) for o in range(ctx)],
        [me, incoming, weight_gate[0], weight_up[0]],
        scratch=[
            pltpu.VMEM((exp * pad, slice_width), BF16),
            pltpu.VMEM((ctx * slots, slice_width), BF16),
        ],
        us=4,
    )
    terms, rest = lax.optimization_barrier((terms, rest))
    downs.update(zip((o for o in range(1, ctx) if o & (o - 1)), rest, strict=True))
    downs = [downs[o] for o in range(ctx)]
    terms = sum_own(terms)

    grad_rows, after_low = run(
        functools.partial(grad_values_kernel, heads, capacity, scale),
        [
            shape((exp, slots, part_width), BF16),
            shape((span // BLOCK * heads, HEAD_DIM, part_width // heads), BF16),
        ],
        [query, key, grad_out, *after_in],
        scratch=[pltpu.VMEM((span, part_width), BF16)],
        us=3,
    )
    grad_rows = move(grad_rows, "exp")

    grads, active = run(
        functools.partial(gates_kernel, len(terms)),
        [shape((slots, 2 * hidden), BF16), shape((slots, hidden), BF16)],
        [me, grad_rows, *terms, *downs],
        scratch=[pltpu.VMEM((slots, width), BF16)], us=0)
    chunks = {0: grads, **{d: swap(grads, d) for d in reversed(doubling)}}
    (expert_out,) = run(
        forward_kernel,
        [shape((exp, slots, part_width), BF16)],
        [me, active, *downs], us=0)
    grad_key, query_part, state = run(
        functools.partial(grad_heads_kernel, heads, capacity, scale),
        [shape((span, key_width), BF16), shape((span, key_width), F32), state_low],
        [query, key, grad_out, after_low, move(expert_out, "exp")], us=0)
    state_in = [
        lax.ppermute(state, CTX, [(i, i + step) for i in range(ctx - step)]) for step in range(1, ctx)
    ]
    far = doubling[-1]
    chunks[far], state_in = lax.optimization_barrier((chunks[far], state_in))
    chunks = spread_rest(chunks, doubling)
    chunks = [chunks[o] for o in range(ctx)]
    (outgoing,) = run(
        functools.partial(backward_kernel, ctx, exp, capacity, pad),
        [shape((ctx * exp, capacity, slice_width), BF16)],
        [me, weight_gate[0], weight_up[0], *chunks],
        scratch=[pltpu.VMEM((ctx * slots, 2 * hidden), BF16)],
        us=60,
    )
    (heads_back,) = run(
        functools.partial(finish_kernel, heads, scale),
        [shape((2 * exp, rows, key_width), BF16)],
        [grad_out, query_part, grad_key, *state_in],
        us=0,
    )
    heads_back = move(heads_back.reshape(exp, 2 * rows, key_width), "exp")
    home = move(outgoing, ALL)
    grad_queries, grad_keys = run(
        functools.partial(heads_kernel, group), [shape((rows, width), BF16)] * 2, [heads_back]
    )
    (grad_tokens,) = run(
        functools.partial(home_kernel, ctx, exp, capacity, pad),
        [shape((rows, width), BF16)],
        [expert_ids, gate_weights, home],
        scratch=[pltpu.VMEM((exp * pad, width), BF16)],
    )
    return grad_tokens, grad_queries, grad_keys


def solution(mesh):
    ctx, exp = mesh.shape["ctx"], mesh.shape["exp"]
    lo = 2 if ctx % 2 == 0 else 1
    split = Mesh(mesh.devices.reshape(ctx // lo, lo, exp), ("hi", "lo", "exp"))
    rows, span = P(("hi", "lo", "exp"), None), ("hi", "lo")
    in_specs = (
        rows,
        rows,
        rows,
        P("exp", span, None),
        P("exp", span, None),
        P("exp", None, span),
        rows,
        rows,
        P(span, "exp"),
    )
    return jax.shard_map(
        shards, mesh=split, in_specs=in_specs, out_specs=(rows, rows, rows), check_vma=False
    )
```

time: 273 us -> 240 us (0.88)
  blocking collectives: 0 us -> 56.2 us
  matrix products: 42.7 us -> 0 us
  Pallas kernels: 0 us -> 23.6 us
  local copies, waits for them, and re-layouts: 27.5 us -> 7.11 us
  starting transfers between devices: 57.1 us -> 41.6 us
  between operations: 14.6 us -> 0.8 us
  other arithmetic: 10.7 us -> 0.18 us
  waiting for transfers between devices: 119 us -> 109 us
    all_to_all x0 -> x4, blocking collectives: none -> 56.2 us  [move(): return lax.all_to_all(buffer, axes, split_axis=0, concat_axis=0, tiled=True)]
    all_to_all x9 -> x3, waiting for transfers between devices: 87.2 us -> 38.4 us  [move(): return lax.all_to_all(buffer, axes, split_axis=0, concat_axis=0, tiled=True)]
    dot_general x26 -> x0, matrix products: 42.7 us -> none  [the longest x9 17 us: contract_rows(): lax.dot_general(left, right, (((1,), (1,)), ((), ())), preferred_element_...]
    ppermute x12 -> x15, waiting for transfers between devices: 31 us -> 70.7 us  [the longest x9 64.9 us: swap(): return lax.ppermute(block, CTX, [(i, i ^ distance) for i in range(count)])]
    pallas_call x0 -> x11, Pallas kernels: none -> 23.6 us  [run(): pl.pallas_call(kernel, out_shape=tuple(outs), in_specs=in_specs, out_spec...]
    all_to_all x9 -> x3, starting transfers between devices: 37.6 us -> 14.1 us  [move(): return lax.all_to_all(buffer, axes, split_axis=0, concat_axis=0, tiled=True)]
    reshape x12 -> x0, local copies, waits for them, and re-layouts: 12.7 us -> none  [the longest x2 2.76 us: heads_in(): array.reshape(row_count, model_width // key_width, key_width)]
    ppermute x12 -> x15, starting transfers between devices: 19.5 us -> 27.5 us  [the longest x9 12.8 us: swap(): return lax.ppermute(block, CTX, [(i, i ^ distance) for i in range(count)])]
  transfers between devices with their start and end apart: 22 -> 18, of which waited for: 12 -> 13; matrix products, arithmetic and copies ran while one was open for 27% -> 1% of each run, Pallas kernels for 0% -> 8%
where the time goes in v2:
time: 240 us; the launch traced here: 239 us
  waiting for transfers between devices  109 us (45%)
  blocking collectives  56.2 us (23%)
  starting transfers between devices  41.6 us (17%)
  Pallas kernels  23.6 us (10%)
  local copies, waits for them, and re-layouts  7.11 us (3%)
    ppermute x9, waiting for transfers between devices, swap(): return lax.ppermute(block, CTX, [(i, i ^ distance) for i in range(count)])  64.9 us
    all_to_all x4, blocking collectives, move(): return lax.all_to_all(buffer, axes, split_axis=0, concat_axis=0, tiled=True)  56.2 us
    all_to_all x3, waiting for transfers between devices, move(): return lax.all_to_all(buffer, axes, split_axis=0, concat_axis=0, tiled=True)  38.4 us
    pallas_call x11, Pallas kernels, run(): pl.pallas_call(kernel, out_shape=tuple(outs), in_specs=in_specs, out_spec...  23.6 us
    all_to_all x3, starting transfers between devices, move(): return lax.all_to_all(buffer, axes, split_axis=0, concat_axis=0, tiled=True)  14.1 us
    ppermute x9, starting transfers between devices, swap(): return lax.ppermute(block, CTX, [(i, i ^ distance) for i in range(count)])  12.8 us
    ppermute x3, starting transfers between devices, shards(): lax.ppermute(state, CTX, [(i, i + step) for i in range(ctx - step)])  10.7 us
    unnamed x24, local copies, waits for them, and re-layouts  7.11 us
  transfers between devices with their start and end apart: 18, of which 13 were waited for; matrix products, arithmetic and copies ran while one was open for 1% of the time, Pallas kernels for 8%

profile of v2, /device:TPU:0, one launch (start us, length us, event | category | flops | bytes accessed | tf_op | source)
XLA Modules:
  0.0 238.6 jit_solution(8722377445045223969)
XLA Ops:
  0.6 3.1 %collective-permute-start = (bf16[1024,512]{1,0:T(8,128)(2,1)}, bf16[1024,512]{1,0:T(8,128)(2,1)S(1)}, u32[]{:S(2)}, u32[]{:S(2)}) collective-permute-start(bf16[1024,512]{1,0:T(8,128)(2,1)} %bitcast.6), channel_id=1, source_target_pairs={{0,8},{8,0},{16,24},{24,16},{1,9},{9,1},{17,25},{25,17},{2,10},{10... | collective-permute-start | bytes 3145736 | tf_op jit(solution)/shard_map/ppermute | solution.py:335
  3.7 2.6 %collective-permute-start.1 = (bf16[1024,512]{1,0:T(8,128)(2,1)}, bf16[1024,512]{1,0:T(8,128)(2,1)S(1)}, u32[]{:S(2)}, u32[]{:S(2)}) collective-permute-start(bf16[1024,512]{1,0:T(8,128)(2,1)} %bitcast.7), channel_id=1, source_target_pairs={{0,16},{8,24},{16,0},{24,8},{1,17},{9,25},{17,1},{25,9},{2,18},{10... | collective-permute-start | bytes 3145736 | tf_op jit(solution)/shard_map/ppermute | solution.py:335
  11.0 1.7 shard_map.112
  12.7 13.4 %all_to_all.35 = bf16[8,128,256]{2,1,0:T(8,128)(2,1)} all-to-all(bf16[8,128,256]{2,1,0:T(8,128)(2,1)S(1)} %get-tuple-element.35), channel_id=1, replica_groups=mesh['hi'=2,'lo'=2,'exp'=8] {'exp'}, dimensions={0} | all-to-all | bytes 1048576 | tf_op jit(solution)/shard_map/all_to_all | solution.py:326
  26.0 13.5 %all_to_all.36.key_ref = bf16[8,144,256]{2,1,0:T(8,128)(2,1)} all-to-all(bf16[8,144,256]{2,1,0:T(8,128)(2,1)S(1)} %get-tuple-element.38), channel_id=1, replica_groups=mesh['hi'=2,'lo'=2,'exp'=8] {'exp'}, dimensions={0} | all-to-all | bytes 1179648 | tf_op jit(solution)/shard_map/all_to_all | solution.py:326
  39.5 9.9 %collective-permute-done.rest_4_.rest_1_ = bf16[1024,512]{1,0:T(8,128)(2,1)S(1)} collective-permute-done((bf16[1024,512]{1,0:T(8,128)(2,1)}, bf16[1024,512]{1,0:T(8,128)(2,1)S(1)}, u32[]{:S(2)}, u32[]{:S(2)}) %collective-permute-start) | collective-permute-done | bytes 1048608 | tf_op jit(solution)/shard_map/ppermute | solution.py:335
  49.4 2.5 %collective-permute-done.1.rest_5_.rest_2_ = bf16[1024,512]{1,0:T(8,128)(2,1)S(1)} collective-permute-done((bf16[1024,512]{1,0:T(8,128)(2,1)}, bf16[1024,512]{1,0:T(8,128)(2,1)S(1)}, u32[]{:S(2)}, u32[]{:S(2)}) %collective-permute-start.1) | collective-permute-done | bytes 1048608 | tf_op jit(solution)/shard_map/ppermute | solution.py:335
  52.0 4.8 %all-to-all-start.3 = ((bf16[32,20,512]{2,1,0:T(8,128)(2,1)}), bf16[32,20,512]{2,1,0:T(8,128)(2,1)}, u32[]{:S(2)}, u32[]{:S(2)}) async-start(bf16[32,20,512]{2,1,0:T(8,128)(2,1)} %get-tuple-element.41), calls=%async_computation.3 | async-start | bytes 1572864 | tf_op jit(solution)/shard_map/all_to_all | solution.py:326
  56.8 1.8 collective-permute-start.5
  58.6 18.9 %all-to-all-done.3.in_ref = bf16[32,20,512]{2,1,0:T(8,128)(2,1)} async-done(((bf16[32,20,512]{2,1,0:T(8,128)(2,1)}), bf16[32,20,512]{2,1,0:T(8,128)(2,1)}, u32[]{:S(2)}, u32[]{:S(2)}) %all-to-all-start.3) | async-done | bytes 655392 | tf_op jit(solution)/shard_map/all_to_all | solution.py:326
  79.9 2.9 %shard_map.115 = (f32[160,2048]{1,0:T(8,128)S(1)}, bf16[160,2048]{1,0:T(8,128)(2,1)S(1)}, f32[160,2048]{1,0:T(8,128)S(1)}, bf16[160,2048]{1,0:T(8,128)(2,1)S(1)}) custom-call(s32[1]{0:T(128)} %bitcast.me_ref, bf16[32,20,512]{2,1,0:T(8,128)(2,1)} %all-to-all-done.3.in_ref, bf16[512,1024]{1,0:T(8,128)(2,1)S(1)} %bitcast.13, bf16[512,1024]{1,0:T(8,128)(2,1)S(1)} %bitcast.15), custom_call_target="tpu_custom_call" | custom-call | flops 4600000000 | bytes 66846 | tf_op jit(solution)/shard_map/pallas_call | solution.py:42
  82.9 11.8 %collective-permute-done.5.rest_6_.rest_3_ = bf16[1024,512]{1,0:T(8,128)(2,1)S(1)} collective-permute-done((bf16[1024,512]{1,0:T(8,128)(2,1)S(1)}, bf16[1024,512]{1,0:T(8,128)(2,1)S(1)}, u32[]{:S(2)}, u32[]{:S(2)}) %collective-permute-start.5) | collective-permute-done | bytes 1048608 | tf_op jit(solution)/shard_map/ppermute | solution.py:335
  99.4 2.1 collective-permute-start.6
  101.5 12.2 %collective-permute-done.7 = bf16[160,2048]{1,0:T(8,128)(2,1)S(1)} collective-permute-done((bf16[160,2048]{1,0:T(8,128)(2,1)S(1)}, bf16[160,2048]{1,0:T(8,128)(2,1)S(1)}, u32[]{:S(2)}, u32[]{:S(2)}) %collective-permute-start.7) | collective-permute-done | bytes 655392 | tf_op jit(solution)/shard_map/ppermute | solution.py:335
  115.0 1.8 collective-permute-done.2.rest_0_
  116.8 1.7 collective-permute-done.4.rest_2_
  118.4 2.7 %shard_map.114 = (bf16[8,160,256]{2,1,0:T(8,128)(2,1)S(1)}, bf16[4,128,128]{2,1,0:T(8,128)(2,1)S(1)}) custom-call(bf16[1024,256]{1,0:T(8,128)(2,1)S(1)} %bitcast.11, bf16[8,144,256]{2,1,0:T(8,128)(2,1)S(1)} %copy-done.1, bf16[1024,256]{1,0:T(8,128)(2,1)S(1)} %copy-done.2, bf16[2,128,128]{2,1,0:T(8,128)(2,1)S(1)} %collective-permute-done.2.rest_0_, ...), custom_call_target="tpu_custom_call" | custom-call | flops 3449999872 | bytes 26214 | tf_op jit(solution)/shard_map/pallas_call | solution.py:42
  121.1 14.8 %all_to_all.37.grads_ref = bf16[8,160,256]{2,1,0:T(8,128)(2,1)S(1)} all-to-all(bf16[8,160,256]{2,1,0:T(8,128)(2,1)S(1)} %get-tuple-element.40), channel_id=1, replica_groups=mesh['hi'=2,'lo'=2,'exp'=8] {'exp'}, dimensions={0} | all-to-all | bytes 1310720 | tf_op jit(solution)/shard_map/all_to_all | solution.py:326
  135.9 7.4 %collective-permute-done.6.rest_1_ = bf16[160,2048]{1,0:T(8,128)(2,1)S(1)} collective-permute-done((bf16[160,2048]{1,0:T(8,128)(2,1)S(1)}, bf16[160,2048]{1,0:T(8,128)(2,1)S(1)}, u32[]{:S(2)}, u32[]{:S(2)}) %collective-permute-start.6) | collective-permute-done | bytes 655392 | tf_op jit(solution)/shard_map/ppermute | solution.py:335
  143.3 2.6 %shard_map.116 = (bf16[160,2048]{1,0:T(8,128)(2,1)}, bf16[160,1024]{1,0:T(8,128)(2,1)S(1)}) custom-call(s32[1]{0:T(128)} %bitcast.me_ref, bf16[8,160,256]{2,1,0:T(8,128)(2,1)S(1)} %all_to_all.37.grads_ref, f32[160,2048]{1,0:T(8,128)S(1)} %get-tuple-element.47.rest_0_, bf16[160,2048]{1,0:T(8,128)(2,1)S(1)} %collective-permute-done.6.rest_1_, ...), custom_call_target="tpu_custom_call" | custom-call | bytes 84541 | tf_op jit(solution)/shard_map/pallas_call | solution.py:42
  146.8 14.6 %all_to_all.38.in_ref = bf16[8,160,256]{2,1,0:T(8,128)(2,1)S(1)} all-to-all(bf16[8,160,256]{2,1,0:T(8,128)(2,1)S(1)} %shard_map.117), channel_id=1, replica_groups=mesh['hi'=2,'lo'=2,'exp'=8] {'exp'}, dimensions={0} | all-to-all | bytes 1310720 | tf_op jit(solution)/shard_map/all_to_all | solution.py:326
  161.4 4.2 %shard_map.118 = (bf16[1024,256]{1,0:T(8,128)(2,1)S(1)}, f32[1024,256]{1,0:T(8,128)S(1)}, bf16[2,128,128]{2,1,0:T(8,128)(2,1)S(1)}) custom-call(bf16[1024,256]{1,0:T(8,128)(2,1)S(1)} %bitcast.12, bf16[8,144,256]{2,1,0:T(8,128)(2,1)S(1)} %copy-done.1, bf16[1024,256]{1,0:T(8,128)(2,1)S(1)} %copy-done.2, bf16[4,128,128]{2,1,0:T(8,128)(2,1)S(1)} %get-tuple-element.54.low_ref, ...), custom_call_target="tpu_custom_call" | custom-call | bytes 40632 | tf_op jit(solution)/shard_map/pallas_call | solution.py:42
  165.6 4.4 %collective-permute-start.11 = (bf16[2,128,128]{2,1,0:T(8,128)(2,1)S(1)}, bf16[2,128,128]{2,1,0:T(8,128)(2,1)S(1)}, u32[]{:S(2)}, u32[]{:S(2)}) collective-permute-start(bf16[2,128,128]{2,1,0:T(8,128)(2,1)S(1)} %get-tuple-element.56), channel_id=1, source_target_pairs={{0,8},{8,16},{16,24},{1,9},{9,17},{17,25},{2,10},{10,18},{18,26},{... | collective-permute-start | bytes 196616 | tf_op jit(solution)/shard_map/ppermute | solution.py:460
  169.9 4.8 %collective-permute-start.12 = (bf16[2,128,128]{2,1,0:T(8,128)(2,1)S(1)}, bf16[2,128,128]{2,1,0:T(8,128)(2,1)S(1)}, u32[]{:S(2)}, u32[]{:S(2)}) collective-permute-start(bf16[2,128,128]{2,1,0:T(8,128)(2,1)S(1)} %get-tuple-element.56), channel_id=1, source_target_pairs={{0,16},{8,24},{1,17},{9,25},{2,18},{10,26},{3,19},{11,27},{4,20},{... | collective-permute-start | bytes 196616 | tf_op jit(solution)/shard_map/ppermute | solution.py:460
  174.8 1.5 collective-permute-start.13
  178.7 1.8 collective-permute-start.14
  181.8 3.8 %all-to-all-start.6 = ((bf16[8,256,256]{2,1,0:T(8,128)(2,1)}), bf16[8,256,256]{2,1,0:T(8,128)(2,1)S(1)}, u32[]{:S(2)}, u32[]{:S(2)}) async-start(bf16[8,256,256]{2,1,0:T(8,128)(2,1)} %bitcast.5), calls=%async_computation.6 | async-start | bytes 2097152 | tf_op jit(solution)/shard_map/all_to_all | solution.py:326
  185.5 8.8 %collective-permute-done.9.rest_1_ = bf16[160,2048]{1,0:T(8,128)(2,1)} collective-permute-done((bf16[160,2048]{1,0:T(8,128)(2,1)}, bf16[160,2048]{1,0:T(8,128)(2,1)}, u32[]{:S(2)}, u32[]{:S(2)}) %collective-permute-start.9) | collective-permute-done | bytes 655392 | tf_op jit(solution)/shard_map/ppermute | solution.py:335
  194.3 12.3 %collective-permute-done.14.rest_3_ = bf16[160,2048]{1,0:T(8,128)(2,1)} collective-permute-done((bf16[160,2048]{1,0:T(8,128)(2,1)}, bf16[160,2048]{1,0:T(8,128)(2,1)}, u32[]{:S(2)}, u32[]{:S(2)}) %collective-permute-start.14) | collective-permute-done | bytes 655392 | tf_op jit(solution)/shard_map/ppermute | solution.py:335
  206.6 4.4 %shard_map.119 = bf16[32,20,512]{2,1,0:T(8,128)(2,1)} custom-call(s32[1]{0:T(128)} %bitcast.me_ref, bf16[512,1024]{1,0:T(8,128)(2,1)S(1)} %bitcast.14, bf16[512,1024]{1,0:T(8,128)(2,1)S(1)} %bitcast.16, bf16[160,2048]{1,0:T(8,128)(2,1)} %get-tuple-element.53.rest_0_, bf16[160,2048]{1,0:T(8,128)(2,1)} %collective-permute-done.9.rest_1_, ...), custom_call_target="tpu_custom_call" | custom-call | flops 69000003584 | bytes 53739 | tf_op jit(solution)/shard_map/pallas_call | solution.py:42
  211.1 5.5 %all-to-all-start.5 = ((bf16[32,20,512]{2,1,0:T(8,128)(2,1)}), bf16[32,20,512]{2,1,0:T(8,128)(2,1)S(1)}, u32[]{:S(2)}, u32[]{:S(2)}) async-start(bf16[32,20,512]{2,1,0:T(8,128)(2,1)} %shard_map.119), calls=%async_computation.5 | async-start | bytes 1572864 | tf_op jit(solution)/shard_map/all_to_all | solution.py:326
  217.7 19.5 %all-to-all-done.5.in_ref = bf16[32,20,512]{2,1,0:T(8,128)(2,1)S(1)} async-done(((bf16[32,20,512]{2,1,0:T(8,128)(2,1)}), bf16[32,20,512]{2,1,0:T(8,128)(2,1)S(1)}, u32[]{:S(2)}, u32[]{:S(2)}) %all-to-all-start.5) | async-done | bytes 655392 | tf_op jit(solution)/shard_map/all_to_all | solution.py:326
  (44 shorter events, 20.2 us)
Async XLA Ops:
  0.6 48.8 %collective-permute-start = (bf16[1024,512]{1,0:T(8,128)(2,1)}, bf16[1024,512]{1,0:T(8,128)(2,1)S(1)}, u32[]{:S(2)}, u32[]{:S(2)}) collective-permute-start(bf16[1024,512]{1,0:T(8,128)(2,1)} %bitcast.6), channel_id=1, source_target_pairs={{0,8},{8,0},{16,24},{24,16},{1,9},{9,1},{17,25},{25,17},{2,10},{10... | collective-permute-start | bytes 3145736 | tf_op jit(solution)/shard_map/ppermute | solution.py:335
  3.7 48.3 %collective-permute-start.1 = (bf16[1024,512]{1,0:T(8,128)(2,1)}, bf16[1024,512]{1,0:T(8,128)(2,1)S(1)}, u32[]{:S(2)}, u32[]{:S(2)}) collective-permute-start(bf16[1024,512]{1,0:T(8,128)(2,1)} %bitcast.7), channel_id=1, source_target_pairs={{0,16},{8,24},{16,0},{24,8},{1,17},{9,25},{17,1},{25,9},{2,18},{10... | collective-permute-start | bytes 3145736 | tf_op jit(solution)/shard_map/ppermute | solution.py:335
  7.8 1.0 copy-start.8
  8.9 1.0 copy-start.9
  9.9 1.0 copy-start.10
  52.0 25.5 %all-to-all-start.3 = ((bf16[32,20,512]{2,1,0:T(8,128)(2,1)}), bf16[32,20,512]{2,1,0:T(8,128)(2,1)}, u32[]{:S(2)}, u32[]{:S(2)}) async-start(bf16[32,20,512]{2,1,0:T(8,128)(2,1)} %get-tuple-element.41), calls=%async_computation.3 | async-start | bytes 1572864 | tf_op jit(solution)/shard_map/all_to_all | solution.py:326
  56.8 37.9 %collective-permute-start.5 = (bf16[1024,512]{1,0:T(8,128)(2,1)S(1)}, bf16[1024,512]{1,0:T(8,128)(2,1)S(1)}, u32[]{:S(2)}, u32[]{:S(2)}) collective-permute-start(bf16[1024,512]{1,0:T(8,128)(2,1)S(1)} %collective-permute-done.1.rest_5_.rest_2_), channel_id=1, source_target_pairs={{0,8},{8,0},{16,24},{24,16},{1,9},{9,1},{17,25},{25,17},{2,10},{10... | collective-permute-start | bytes 3145736 | tf_op jit(solution)/shard_map/ppermute | solution.py:335
  77.5 1.2 copy-start.4
  78.7 1.2 copy-start.6
  79.9 15.1 %copy-start.2 = (bf16[1024,256]{1,0:T(8,128)(2,1)S(1)}, bf16[1024,256]{1,0:T(8,128)(2,1)}, u32[]{:S(2)}) copy-start(bf16[1024,256]{1,0:T(8,128)(2,1)} %cot_ref.7) | copy-start | bytes 1572868
  79.9 15.1 %copy-start.3 = (bf16[8,128,256]{2,1,0:T(8,128)(2,1)S(1)}, bf16[8,128,256]{2,1,0:T(8,128)(2,1)}, u32[]{:S(2)}) copy-start(bf16[8,128,256]{2,1,0:T(8,128)(2,1)} %all_to_all.35) | copy-start | bytes 1572868
  94.7 19.1 %collective-permute-start.7 = (bf16[160,2048]{1,0:T(8,128)(2,1)S(1)}, bf16[160,2048]{1,0:T(8,128)(2,1)S(1)}, u32[]{:S(2)}, u32[]{:S(2)}) collective-permute-start(bf16[160,2048]{1,0:T(8,128)(2,1)S(1)} %get-tuple-element.50), channel_id=1, source_target_pairs={{0,8},{8,0},{16,24},{24,16},{1,9},{9,1},{17,25},{25,17},{2,10},{10... | collective-permute-start | bytes 1966088 | tf_op jit(solution)/shard_map/ppermute | solution.py:335
  95.4 23.1 %copy-start.1 = (bf16[8,144,256]{2,1,0:T(8,128)(2,1)S(1)}, bf16[8,144,256]{2,1,0:T(8,128)(2,1)}, u32[]{:S(2)}) copy-start(bf16[8,144,256]{2,1,0:T(8,128)(2,1)} %all_to_all.36.key_ref) | copy-start | bytes 1769476
  95.4 21.4 %collective-permute-start.2 = (bf16[2,128,128]{2,1,0:T(8,128)(2,1)S(1)}, bf16[2,128,128]{2,1,0:T(8,128)(2,1)S(1)}, u32[]{:S(2)}, u32[]{:S(2)}) collective-permute-start(bf16[2,128,128]{2,1,0:T(8,128)(2,1)S(1)} %shard_map.113), channel_id=1, source_target_pairs={{8,0},{16,8},{24,16},{9,1},{17,9},{25,17},{10,2},{18,10},{26,18},{... | collective-permute-start | bytes 196616 | tf_op jit(solution)/shard_map/ppermute | solution.py:410
  96.8 19.9 %collective-permute-start.3 = (bf16[2,128,128]{2,1,0:T(8,128)(2,1)S(1)}, bf16[2,128,128]{2,1,0:T(8,128)(2,1)S(1)}, u32[]{:S(2)}, u32[]{:S(2)}) collective-permute-start(bf16[2,128,128]{2,1,0:T(8,128)(2,1)S(1)} %shard_map.113), channel_id=1, source_target_pairs={{16,0},{24,8},{17,1},{25,9},{18,2},{26,10},{19,3},{27,11},{20,4},{... | collective-permute-start | bytes 196616 | tf_op jit(solution)/shard_map/ppermute | solution.py:410
  98.1 20.3 %collective-permute-start.4 = (bf16[2,128,128]{2,1,0:T(8,128)(2,1)S(1)}, bf16[2,128,128]{2,1,0:T(8,128)(2,1)S(1)}, u32[]{:S(2)}, u32[]{:S(2)}) collective-permute-start(bf16[2,128,128]{2,1,0:T(8,128)(2,1)S(1)} %shard_map.113), channel_id=1, source_target_pairs={{24,0},{25,1},{26,2},{27,3},{28,4},{29,5},{30,6},{31,7}} | collective-permute-start | bytes 196616 | tf_op jit(solution)/shard_map/ppermute | solution.py:410
  99.4 43.8 %collective-permute-start.6 = (bf16[160,2048]{1,0:T(8,128)(2,1)S(1)}, bf16[160,2048]{1,0:T(8,128)(2,1)S(1)}, u32[]{:S(2)}, u32[]{:S(2)}) collective-permute-start(bf16[160,2048]{1,0:T(8,128)(2,1)S(1)} %get-tuple-element.48), channel_id=1, source_target_pairs={{0,8},{8,0},{16,24},{24,16},{1,9},{9,1},{17,25},{25,17},{2,10},{10... | collective-permute-start | bytes 1966088 | tf_op jit(solution)/shard_map/ppermute | solution.py:335
  113.9 29.3 %collective-permute-start.8 = (bf16[160,2048]{1,0:T(8,128)(2,1)S(1)}, bf16[160,2048]{1,0:T(8,128)(2,1)S(1)}, u32[]{:S(2)}, u32[]{:S(2)}) collective-permute-start(bf16[160,2048]{1,0:T(8,128)(2,1)S(1)} %add_convert_fusion), channel_id=1, source_target_pairs={{0,16},{8,24},{16,0},{24,8},{1,17},{9,25},{17,1},{25,9},{2,18},{10... | collective-permute-start | bytes 1966088 | tf_op jit(solution)/shard_map/ppermute | solution.py:335
  121.1 22.1 %copy-start = (bf16[1,1024,512]{2,1,0:T(8,128)(2,1)S(1)}, bf16[1,1024,512]{2,1,0:T(8,128)(2,1)}, u32[]{:S(2)}) copy-start(bf16[1,1024,512]{2,1,0:T(8,128)(2,1)} %param.14) | copy-start | bytes 3145732
  145.9 32.8 %collective-permute-start.10 = (bf16[160,2048]{1,0:T(8,128)(2,1)}, bf16[160,2048]{1,0:T(8,128)(2,1)}, u32[]{:S(2)}, u32[]{:S(2)}) collective-permute-start(bf16[160,2048]{1,0:T(8,128)(2,1)} %get-tuple-element.53.rest_0_), channel_id=1, source_target_pairs={{0,16},{8,24},{16,0},{24,8},{1,17},{9,25},{17,1},{25,9},{2,18},{10... | collective-permute-start | bytes 1966088 | tf_op jit(solution)/shard_map/ppermute | solution.py:335
  165.6 10.8 %collective-permute-start.11 = (bf16[2,128,128]{2,1,0:T(8,128)(2,1)S(1)}, bf16[2,128,128]{2,1,0:T(8,128)(2,1)S(1)}, u32[]{:S(2)}, u32[]{:S(2)}) collective-permute-start(bf16[2,128,128]{2,1,0:T(8,128)(2,1)S(1)} %get-tuple-element.56), channel_id=1, source_target_pairs={{0,8},{8,16},{16,24},{1,9},{9,17},{17,25},{2,10},{10,18},{18,26},{... | collective-permute-start | bytes 196616 | tf_op jit(solution)/shard_map/ppermute | solution.py:460
  169.9 7.3 %collective-permute-start.12 = (bf16[2,128,128]{2,1,0:T(8,128)(2,1)S(1)}, bf16[2,128,128]{2,1,0:T(8,128)(2,1)S(1)}, u32[]{:S(2)}, u32[]{:S(2)}) collective-permute-start(bf16[2,128,128]{2,1,0:T(8,128)(2,1)S(1)} %get-tuple-element.56), channel_id=1, source_target_pairs={{0,16},{8,24},{1,17},{9,25},{2,18},{10,26},{3,19},{11,27},{4,20},{... | collective-permute-start | bytes 196616 | tf_op jit(solution)/shard_map/ppermute | solution.py:460
  174.8 3.9 %collective-permute-start.13 = (bf16[2,128,128]{2,1,0:T(8,128)(2,1)S(1)}, bf16[2,128,128]{2,1,0:T(8,128)(2,1)S(1)}, u32[]{:S(2)}, u32[]{:S(2)}) collective-permute-start(bf16[2,128,128]{2,1,0:T(8,128)(2,1)S(1)} %get-tuple-element.56), channel_id=1, source_target_pairs={{0,24},{1,25},{2,26},{3,27},{4,28},{5,29},{6,30},{7,31}} | collective-permute-start | bytes 196616 | tf_op jit(solution)/shard_map/ppermute | solution.py:460
  176.3 18.1 %collective-permute-start.9 = (bf16[160,2048]{1,0:T(8,128)(2,1)}, bf16[160,2048]{1,0:T(8,128)(2,1)}, u32[]{:S(2)}, u32[]{:S(2)}) collective-permute-start(bf16[160,2048]{1,0:T(8,128)(2,1)} %get-tuple-element.53.rest_0_), channel_id=1, source_target_pairs={{0,8},{8,0},{16,24},{24,16},{1,9},{9,1},{17,25},{25,17},{2,10},{10... | collective-permute-start | bytes 1966088 | tf_op jit(solution)/shard_map/ppermute | solution.py:335
  178.7 27.9 %collective-permute-start.14 = (bf16[160,2048]{1,0:T(8,128)(2,1)}, bf16[160,2048]{1,0:T(8,128)(2,1)}, u32[]{:S(2)}, u32[]{:S(2)}) collective-permute-start(bf16[160,2048]{1,0:T(8,128)(2,1)} %collective-permute-done.10.rest_2_), channel_id=1, source_target_pairs={{0,8},{8,0},{16,24},{24,16},{1,9},{9,1},{17,25},{25,17},{2,10},{10... | collective-permute-start | bytes 1966088 | tf_op jit(solution)/shard_map/ppermute | solution.py:335
  181.8 24.9 %copy-start.5 = (bf16[1,512,1024]{2,1,0:T(8,128)(2,1)S(1)}, bf16[1,512,1024]{2,1,0:T(8,128)(2,1)}, u32[]{:S(2)}) copy-start(bf16[1,512,1024]{2,1,0:T(8,128)(2,1)} %param.12) | copy-start | bytes 3145732
  181.8 24.9 %copy-start.7 = (bf16[1,512,1024]{2,1,0:T(8,128)(2,1)S(1)}, bf16[1,512,1024]{2,1,0:T(8,128)(2,1)}, u32[]{:S(2)}) copy-start(bf16[1,512,1024]{2,1,0:T(8,128)(2,1)} %param.13) | copy-start | bytes 3145732
  181.8 29.3 %all-to-all-start.6 = ((bf16[8,256,256]{2,1,0:T(8,128)(2,1)}), bf16[8,256,256]{2,1,0:T(8,128)(2,1)S(1)}, u32[]{:S(2)}, u32[]{:S(2)}) async-start(bf16[8,256,256]{2,1,0:T(8,128)(2,1)} %bitcast.5), calls=%async_computation.6 | async-start | bytes 2097152 | tf_op jit(solution)/shard_map/all_to_all | solution.py:326
  211.1 26.1 %all-to-all-start.5 = ((bf16[32,20,512]{2,1,0:T(8,128)(2,1)}), bf16[32,20,512]{2,1,0:T(8,128)(2,1)S(1)}, u32[]{:S(2)}, u32[]{:S(2)}) async-start(bf16[32,20,512]{2,1,0:T(8,128)(2,1)} %shard_map.119), calls=%async_computation.5 | async-start | bytes 1572864 | tf_op jit(solution)/shard_map/all_to_all | solution.py:326

commit v3 on v2

--- a/solution.py
+++ b/solution.py
@@ -343,7 +343,7 @@
     return chunks
 
 
-def sum_own(terms):
+def sum_own(terms, rest):
     count, distance = len(terms), 1
     held, own = dict(enumerate(terms)), [terms[0]]
     while distance < count:
@@ -351,12 +351,11 @@
         arrived = {o ^ distance: swap(held[o].astype(BF16), distance) for o in urgent}
         last = held[distance].astype(BF16)
         held = {o: held[o].astype(F32) + term.astype(F32) for o, term in arrived.items()}
-        if held:
-            first = max(held)
-            held[first] = held[first].astype(BF16)
+        if distance == 1:
+            last, rest = lax.optimization_barrier((last, rest))
         own.append(swap(last, distance))
         distance *= 2
-    return own
+    return own, rest
 
 
 def shards(
@@ -425,10 +424,9 @@
         ],
         us=4,
     )
-    terms, rest = lax.optimization_barrier((terms, rest))
+    terms, rest = sum_own(terms, rest)
     downs.update(zip((o for o in range(1, ctx) if o & (o - 1)), rest, strict=True))
     downs = [downs[o] for o in range(ctx)]
-    terms = sum_own(terms)
 
     grad_rows, after_low = run(
         functools.partial(grad_values_kernel, heads, capacity, scale),
@@ -446,21 +444,26 @@
         functools.partial(gates_kernel, len(terms)),
         [shape((slots, 2 * hidden), BF16), shape((slots, hidden), BF16)],
         [me, grad_rows, *terms, *downs],
-        scratch=[pltpu.VMEM((slots, width), BF16)], us=0)
+        scratch=[pltpu.VMEM((slots, width), BF16)],
+        us=0,
+    )
     chunks = {0: grads, **{d: swap(grads, d) for d in reversed(doubling)}}
     (expert_out,) = run(
         forward_kernel,
         [shape((exp, slots, part_width), BF16)],
-        [me, active, *downs], us=0)
+        [me, active, *downs],
+        us=0,
+    )
     grad_key, query_part, state = run(
         functools.partial(grad_heads_kernel, heads, capacity, scale),
         [shape((span, key_width), BF16), shape((span, key_width), F32), state_low],
-        [query, key, grad_out, after_low, move(expert_out, "exp")], us=0)
+        [query, key, grad_out, after_low, move(expert_out, "exp")],
+        us=0,
+    )
     state_in = [
         lax.ppermute(state, CTX, [(i, i + step) for i in range(ctx - step)]) for step in range(1, ctx)
     ]
-    far = doubling[-1]
-    chunks[far], state_in = lax.optimization_barrier((chunks[far], state_in))
+    chunks, state_in = lax.optimization_barrier((chunks, state_in))
     chunks = spread_rest(chunks, doubling)
     chunks = [chunks[o] for o in range(ctx)]
     (outgoing,) = run(

time: 240 us -> 229 us (0.954)
  waiting for transfers between devices: 109 us -> 96.7 us
    ppermute x9, waiting for transfers between devices: 64.9 us -> 52.9 us  [swap(): return lax.ppermute(block, CTX, [(i, i ^ distance) for i in range(count)])]
    ppermute x9, starting transfers between devices: 12.8 us -> 15.4 us  [swap(): return lax.ppermute(block, CTX, [(i, i ^ distance) for i in range(count)])]
    ppermute x3, starting transfers between devices: 10.7 us -> 8.15 us  [shards(): lax.ppermute(state, CTX, [(i, i + step) for i in range(ctx - step)])]
    unnamed x24 -> x32, local copies, waits for them, and re-layouts: 7.11 us -> 9.3 us
  transfers between devices with their start and end apart: 18 -> 18, of which waited for: 13 -> 12; matrix products, arithmetic and copies ran while one was open for 1% -> 1% of each run, Pallas kernels for 8% -> 8%
where the time goes in v3:
time: 229 us; the launch traced here: 228 us
  waiting for transfers between devices  96.7 us (42%)
  blocking collectives  56.3 us (25%)
  starting transfers between devices  42.7 us (19%)
  Pallas kernels  22.4 us (10%)
  local copies, waits for them, and re-layouts  9.3 us (4%)
    all_to_all x4, blocking collectives, move(): return lax.all_to_all(buffer, axes, split_axis=0, concat_axis=0, tiled=True)  56.3 us
    ppermute x9, waiting for transfers between devices, swap(): return lax.ppermute(block, CTX, [(i, i ^ distance) for i in range(count)])  52.9 us
    all_to_all x3, waiting for transfers between devices, move(): return lax.all_to_all(buffer, axes, split_axis=0, concat_axis=0, tiled=True)  38.4 us
    pallas_call x11, Pallas kernels, run(): pl.pallas_call(kernel, out_shape=tuple(outs), in_specs=in_specs, out_spec...  22.4 us
    ppermute x9, starting transfers between devices, swap(): return lax.ppermute(block, CTX, [(i, i ^ distance) for i in range(count)])  15.4 us
    all_to_all x3, starting transfers between devices, move(): return lax.all_to_all(buffer, axes, split_axis=0, concat_axis=0, tiled=True)  15.3 us
    unnamed x32, local copies, waits for them, and re-layouts  9.3 us
    ppermute x3, starting transfers between devices, shards(): lax.ppermute(state, CTX, [(i, i + step) for i in range(ctx - step)])  8.15 us
  transfers between devices with their start and end apart: 18, of which 12 were waited for; matrix products, arithmetic and copies ran while one was open for 1% of the time, Pallas kernels for 8%

profile of v3, /device:TPU:0, one launch (start us, length us, event | category | flops | bytes accessed | tf_op | source)
XLA Modules:
  0.0 228.4 jit_solution(3506445755682203324)
XLA Ops:
  0.6 3.1 %collective-permute-start = (bf16[1024,512]{1,0:T(8,128)(2,1)}, bf16[1024,512]{1,0:T(8,128)(2,1)S(1)}, u32[]{:S(2)}, u32[]{:S(2)}) collective-permute-start(bf16[1024,512]{1,0:T(8,128)(2,1)} %bitcast.6), channel_id=1, source_target_pairs={{0,8},{8,0},{16,24},{24,16},{1,9},{9,1},{17,25},{25,17},{2,10},{10... | collective-permute-start | bytes 3145736 | tf_op jit(solution)/shard_map/ppermute | solution.py:335
  3.7 2.6 %collective-permute-start.1 = (bf16[1024,512]{1,0:T(8,128)(2,1)}, bf16[1024,512]{1,0:T(8,128)(2,1)S(1)}, u32[]{:S(2)}, u32[]{:S(2)}) collective-permute-start(bf16[1024,512]{1,0:T(8,128)(2,1)} %bitcast.7), channel_id=1, source_target_pairs={{0,16},{8,24},{16,0},{24,8},{1,17},{9,25},{17,1},{25,9},{2,18},{10... | collective-permute-start | bytes 3145736 | tf_op jit(solution)/shard_map/ppermute | solution.py:335
  11.0 1.7 shard_map.112
  12.7 13.4 %all_to_all.35 = bf16[8,128,256]{2,1,0:T(8,128)(2,1)} all-to-all(bf16[8,128,256]{2,1,0:T(8,128)(2,1)S(1)} %get-tuple-element.34), channel_id=1, replica_groups=mesh['hi'=2,'lo'=2,'exp'=8] {'exp'}, dimensions={0} | all-to-all | bytes 1048576 | tf_op jit(solution)/shard_map/all_to_all | solution.py:326
  26.0 13.5 %all_to_all.36.key_ref = bf16[8,144,256]{2,1,0:T(8,128)(2,1)} all-to-all(bf16[8,144,256]{2,1,0:T(8,128)(2,1)S(1)} %get-tuple-element.37), channel_id=1, replica_groups=mesh['hi'=2,'lo'=2,'exp'=8] {'exp'}, dimensions={0} | all-to-all | bytes 1179648 | tf_op jit(solution)/shard_map/all_to_all | solution.py:326
  39.5 9.9 %collective-permute-done.rest_4_.rest_1_ = bf16[1024,512]{1,0:T(8,128)(2,1)S(1)} collective-permute-done((bf16[1024,512]{1,0:T(8,128)(2,1)}, bf16[1024,512]{1,0:T(8,128)(2,1)S(1)}, u32[]{:S(2)}, u32[]{:S(2)}) %collective-permute-start) | collective-permute-done | bytes 1048608 | tf_op jit(solution)/shard_map/ppermute | solution.py:335
  49.4 2.5 %collective-permute-done.1.rest_5_.rest_2_ = bf16[1024,512]{1,0:T(8,128)(2,1)S(1)} collective-permute-done((bf16[1024,512]{1,0:T(8,128)(2,1)}, bf16[1024,512]{1,0:T(8,128)(2,1)S(1)}, u32[]{:S(2)}, u32[]{:S(2)}) %collective-permute-start.1) | collective-permute-done | bytes 1048608 | tf_op jit(solution)/shard_map/ppermute | solution.py:335
  52.0 4.8 %all-to-all-start.3 = ((bf16[32,20,512]{2,1,0:T(8,128)(2,1)}), bf16[32,20,512]{2,1,0:T(8,128)(2,1)}, u32[]{:S(2)}, u32[]{:S(2)}) async-start(bf16[32,20,512]{2,1,0:T(8,128)(2,1)} %get-tuple-element.40), calls=%async_computation.3 | async-start | bytes 1572864 | tf_op jit(solution)/shard_map/all_to_all | solution.py:326
  56.8 1.8 collective-permute-start.5
  58.6 18.9 %all-to-all-done.3.in_ref = bf16[32,20,512]{2,1,0:T(8,128)(2,1)} async-done(((bf16[32,20,512]{2,1,0:T(8,128)(2,1)}), bf16[32,20,512]{2,1,0:T(8,128)(2,1)}, u32[]{:S(2)}, u32[]{:S(2)}) %all-to-all-start.3) | async-done | bytes 655392 | tf_op jit(solution)/shard_map/all_to_all | solution.py:326
  79.9 2.9 %shard_map.115 = (f32[160,2048]{1,0:T(8,128)S(1)}, bf16[160,2048]{1,0:T(8,128)(2,1)S(1)}, f32[160,2048]{1,0:T(8,128)S(1)}, bf16[160,2048]{1,0:T(8,128)(2,1)S(1)}) custom-call(s32[1]{0:T(128)} %bitcast.me_ref, bf16[32,20,512]{2,1,0:T(8,128)(2,1)} %all-to-all-done.3.in_ref, bf16[512,1024]{1,0:T(8,128)(2,1)S(1)} %bitcast.13, bf16[512,1024]{1,0:T(8,128)(2,1)S(1)} %bitcast.15), custom_call_target="tpu_custom_call" | custom-call | flops 4600000000 | bytes 66846 | tf_op jit(solution)/shard_map/pallas_call | solution.py:42
  82.9 1.4 collective-permute-start.7
  88.5 8.0 %collective-permute-done.5.rest_6_.rest_3_ = bf16[1024,512]{1,0:T(8,128)(2,1)S(1)} collective-permute-done((bf16[1024,512]{1,0:T(8,128)(2,1)S(1)}, bf16[1024,512]{1,0:T(8,128)(2,1)S(1)}, u32[]{:S(2)}, u32[]{:S(2)}) %collective-permute-start.5) | collective-permute-done | bytes 1048608 | tf_op jit(solution)/shard_map/ppermute | solution.py:335
  96.5 14.0 %collective-permute-done.7 = bf16[160,2048]{1,0:T(8,128)(2,1)S(1)} collective-permute-done((bf16[160,2048]{1,0:T(8,128)(2,1)S(1)}, bf16[160,2048]{1,0:T(8,128)(2,1)S(1)}, u32[]{:S(2)}, u32[]{:S(2)}) %collective-permute-start.7) | collective-permute-done | bytes 655392 | tf_op jit(solution)/shard_map/ppermute | solution.py:335
  112.0 3.3 %collective-permute-done.4.rest_2_ = bf16[2,128,128]{2,1,0:T(8,128)(2,1)S(1)} collective-permute-done((bf16[2,128,128]{2,1,0:T(8,128)(2,1)S(1)}, bf16[2,128,128]{2,1,0:T(8,128)(2,1)S(1)}, u32[]{:S(2)}, u32[]{:S(2)}) %collective-permute-start.4) | collective-permute-done | bytes 65568 | tf_op jit(solution)/shard_map/ppermute | solution.py:409
  115.3 2.7 %shard_map.114 = (bf16[8,160,256]{2,1,0:T(8,128)(2,1)S(1)}, bf16[4,128,128]{2,1,0:T(8,128)(2,1)S(1)}) custom-call(bf16[1024,256]{1,0:T(8,128)(2,1)S(1)} %bitcast.11, bf16[8,144,256]{2,1,0:T(8,128)(2,1)S(1)} %copy-done.1, bf16[1024,256]{1,0:T(8,128)(2,1)S(1)} %copy-done.2, bf16[2,128,128]{2,1,0:T(8,128)(2,1)S(1)} %collective-permute-done.2.rest_0_, ...), custom_call_target="tpu_custom_call" | custom-call | flops 3449999872 | bytes 26214 | tf_op jit(solution)/shard_map/pallas_call | solution.py:42
  118.0 14.8 %all_to_all.37.grads_ref = bf16[8,160,256]{2,1,0:T(8,128)(2,1)S(1)} all-to-all(bf16[8,160,256]{2,1,0:T(8,128)(2,1)S(1)} %get-tuple-element.39), channel_id=1, replica_groups=mesh['hi'=2,'lo'=2,'exp'=8] {'exp'}, dimensions={0} | all-to-all | bytes 1310720 | tf_op jit(solution)/shard_map/all_to_all | solution.py:326
  132.8 8.3 %collective-permute-done.6.rest_1_ = bf16[160,2048]{1,0:T(8,128)(2,1)S(1)} collective-permute-done((bf16[160,2048]{1,0:T(8,128)(2,1)S(1)}, bf16[160,2048]{1,0:T(8,128)(2,1)S(1)}, u32[]{:S(2)}, u32[]{:S(2)}) %collective-permute-start.6) | collective-permute-done | bytes 655392 | tf_op jit(solution)/shard_map/ppermute | solution.py:335
  141.0 1.7 shard_map.116
  142.9 2.5 %collective-permute-start.9 = (bf16[160,2048]{1,0:T(8,128)(2,1)S(1)}, bf16[160,2048]{1,0:T(8,128)(2,1)S(1)}, u32[]{:S(2)}, u32[]{:S(2)}) collective-permute-start(bf16[160,2048]{1,0:T(8,128)(2,1)S(1)} %get-tuple-element.53.rest_0_), channel_id=1, source_target_pairs={{0,8},{8,0},{16,24},{24,16},{1,9},{9,1},{17,25},{25,17},{2,10},{10... | collective-permute-start | bytes 1966088 | tf_op jit(solution)/shard_map/ppermute | solution.py:335
  146.3 14.6 %all_to_all.38.in_ref = bf16[8,160,256]{2,1,0:T(8,128)(2,1)S(1)} all-to-all(bf16[8,160,256]{2,1,0:T(8,128)(2,1)S(1)} %shard_map.117), channel_id=1, replica_groups=mesh['hi'=2,'lo'=2,'exp'=8] {'exp'}, dimensions={0} | all-to-all | bytes 1310720 | tf_op jit(solution)/shard_map/all_to_all | solution.py:326
  160.9 4.2 %shard_map.118 = (bf16[1024,256]{1,0:T(8,128)(2,1)S(1)}, f32[1024,256]{1,0:T(8,128)S(1)}, bf16[2,128,128]{2,1,0:T(8,128)(2,1)S(1)}) custom-call(bf16[1024,256]{1,0:T(8,128)(2,1)S(1)} %bitcast.12, bf16[8,144,256]{2,1,0:T(8,128)(2,1)S(1)} %copy-done.1, bf16[1024,256]{1,0:T(8,128)(2,1)S(1)} %copy-done.2, bf16[4,128,128]{2,1,0:T(8,128)(2,1)S(1)} %get-tuple-element.50.low_ref, ...), custom_call_target="tpu_custom_call" | custom-call | bytes 40632 | tf_op jit(solution)/shard_map/pallas_call | solution.py:42
  165.1 1.9 collective-permute-start.11
  167.0 4.7 %collective-permute-start.12 = (bf16[2,128,128]{2,1,0:T(8,128)(2,1)S(1)}, bf16[2,128,128]{2,1,0:T(8,128)(2,1)S(1)}, u32[]{:S(2)}, u32[]{:S(2)}) collective-permute-start(bf16[2,128,128]{2,1,0:T(8,128)(2,1)S(1)} %get-tuple-element.52), channel_id=1, source_target_pairs={{0,16},{8,24},{1,17},{9,25},{2,18},{10,26},{3,19},{11,27},{4,20},{... | collective-permute-start | bytes 196616 | tf_op jit(solution)/shard_map/ppermute | solution.py:464
  171.8 1.5 collective-permute-start.13
  175.3 2.9 %collective-permute-start.14 = (bf16[160,2048]{1,0:T(8,128)(2,1)}, bf16[160,2048]{1,0:T(8,128)(2,1)}, u32[]{:S(2)}, u32[]{:S(2)}) collective-permute-start(bf16[160,2048]{1,0:T(8,128)(2,1)} %collective-permute-done.10.rest_2_), channel_id=1, source_target_pairs={{0,8},{8,0},{16,24},{24,16},{1,9},{9,1},{17,25},{25,17},{2,10},{10... | collective-permute-start | bytes 1966088 | tf_op jit(solution)/shard_map/ppermute | solution.py:335
  179.5 3.8 %all-to-all-start.6 = ((bf16[8,256,256]{2,1,0:T(8,128)(2,1)}), bf16[8,256,256]{2,1,0:T(8,128)(2,1)S(1)}, u32[]{:S(2)}, u32[]{:S(2)}) async-start(bf16[8,256,256]{2,1,0:T(8,128)(2,1)} %bitcast.5), calls=%async_computation.6 | async-start | bytes 2097152 | tf_op jit(solution)/shard_map/all_to_all | solution.py:326
  183.3 10.1 %collective-permute-done.14.rest_3_ = bf16[160,2048]{1,0:T(8,128)(2,1)} collective-permute-done((bf16[160,2048]{1,0:T(8,128)(2,1)}, bf16[160,2048]{1,0:T(8,128)(2,1)}, u32[]{:S(2)}, u32[]{:S(2)}) %collective-permute-start.14) | collective-permute-done | bytes 655392 | tf_op jit(solution)/shard_map/ppermute | solution.py:335
  195.6 4.0 %shard_map.119 = bf16[32,20,512]{2,1,0:T(8,128)(2,1)} custom-call(s32[1]{0:T(128)} %bitcast.me_ref, bf16[512,1024]{1,0:T(8,128)(2,1)S(1)} %bitcast.14, bf16[512,1024]{1,0:T(8,128)(2,1)S(1)} %bitcast.16, bf16[160,2048]{1,0:T(8,128)(2,1)S(1)} %copy-done.9, bf16[160,2048]{1,0:T(8,128)(2,1)S(1)} %copy-done.11, ...), custom_call_target="tpu_custom_call" | custom-call | flops 69000003584 | bytes 53739 | tf_op jit(solution)/shard_map/pallas_call | solution.py:42
  199.6 6.7 %all-to-all-start.5 = ((bf16[32,20,512]{2,1,0:T(8,128)(2,1)}), bf16[32,20,512]{2,1,0:T(8,128)(2,1)S(1)}, u32[]{:S(2)}, u32[]{:S(2)}) async-start(bf16[32,20,512]{2,1,0:T(8,128)(2,1)} %shard_map.119), calls=%async_computation.5 | async-start | bytes 1572864 | tf_op jit(solution)/shard_map/all_to_all | solution.py:326
  207.4 19.5 %all-to-all-done.5.in_ref = bf16[32,20,512]{2,1,0:T(8,128)(2,1)S(1)} async-done(((bf16[32,20,512]{2,1,0:T(8,128)(2,1)}), bf16[32,20,512]{2,1,0:T(8,128)(2,1)S(1)}, u32[]{:S(2)}, u32[]{:S(2)}) %all-to-all-start.5) | async-done | bytes 655392 | tf_op jit(solution)/shard_map/all_to_all | solution.py:326
  227.0 1.4 shard_map.120
  (52 shorter events, 20.3 us)
Async XLA Ops:
  0.6 48.8 %collective-permute-start = (bf16[1024,512]{1,0:T(8,128)(2,1)}, bf16[1024,512]{1,0:T(8,128)(2,1)S(1)}, u32[]{:S(2)}, u32[]{:S(2)}) collective-permute-start(bf16[1024,512]{1,0:T(8,128)(2,1)} %bitcast.6), channel_id=1, source_target_pairs={{0,8},{8,0},{16,24},{24,16},{1,9},{9,1},{17,25},{25,17},{2,10},{10... | collective-permute-start | bytes 3145736 | tf_op jit(solution)/shard_map/ppermute | solution.py:335
  3.7 48.3 %collective-permute-start.1 = (bf16[1024,512]{1,0:T(8,128)(2,1)}, bf16[1024,512]{1,0:T(8,128)(2,1)S(1)}, u32[]{:S(2)}, u32[]{:S(2)}) collective-permute-start(bf16[1024,512]{1,0:T(8,128)(2,1)} %bitcast.7), channel_id=1, source_target_pairs={{0,16},{8,24},{16,0},{24,8},{1,17},{9,25},{17,1},{25,9},{2,18},{10... | collective-permute-start | bytes 3145736 | tf_op jit(solution)/shard_map/ppermute | solution.py:335
  7.8 1.0 copy-start.12
  8.9 1.0 copy-start.13
  52.0 25.5 %all-to-all-start.3 = ((bf16[32,20,512]{2,1,0:T(8,128)(2,1)}), bf16[32,20,512]{2,1,0:T(8,128)(2,1)}, u32[]{:S(2)}, u32[]{:S(2)}) async-start(bf16[32,20,512]{2,1,0:T(8,128)(2,1)} %get-tuple-element.40), calls=%async_computation.3 | async-start | bytes 1572864 | tf_op jit(solution)/shard_map/all_to_all | solution.py:326
  56.8 39.7 %collective-permute-start.5 = (bf16[1024,512]{1,0:T(8,128)(2,1)S(1)}, bf16[1024,512]{1,0:T(8,128)(2,1)S(1)}, u32[]{:S(2)}, u32[]{:S(2)}) collective-permute-start(bf16[1024,512]{1,0:T(8,128)(2,1)S(1)} %collective-permute-done.1.rest_5_.rest_2_), channel_id=1, source_target_pairs={{0,8},{8,0},{16,24},{24,16},{1,9},{9,1},{17,25},{25,17},{2,10},{10... | collective-permute-start | bytes 3145736 | tf_op jit(solution)/shard_map/ppermute | solution.py:335
  77.5 1.2 copy-start.4
  78.7 1.2 copy-start.6
  79.9 4.3 %copy-start.2 = (bf16[1024,256]{1,0:T(8,128)(2,1)S(1)}, bf16[1024,256]{1,0:T(8,128)(2,1)}, u32[]{:S(2)}) copy-start(bf16[1024,256]{1,0:T(8,128)(2,1)} %cot_ref.7) | copy-start | bytes 1572868
  79.9 4.3 %copy-start.3 = (bf16[8,128,256]{2,1,0:T(8,128)(2,1)S(1)}, bf16[8,128,256]{2,1,0:T(8,128)(2,1)}, u32[]{:S(2)}) copy-start(bf16[8,128,256]{2,1,0:T(8,128)(2,1)} %all_to_all.35) | copy-start | bytes 1572868
  82.9 27.7 %collective-permute-start.7 = (bf16[160,2048]{1,0:T(8,128)(2,1)S(1)}, bf16[160,2048]{1,0:T(8,128)(2,1)S(1)}, u32[]{:S(2)}, u32[]{:S(2)}) collective-permute-start(bf16[160,2048]{1,0:T(8,128)(2,1)S(1)} %get-tuple-element.46), channel_id=1, source_target_pairs={{0,8},{8,0},{16,24},{24,16},{1,9},{9,1},{17,25},{25,17},{2,10},{10... | collective-permute-start | bytes 1966088 | tf_op jit(solution)/shard_map/ppermute | solution.py:335
  84.6 27.4 %collective-permute-start.2 = (bf16[2,128,128]{2,1,0:T(8,128)(2,1)S(1)}, bf16[2,128,128]{2,1,0:T(8,128)(2,1)S(1)}, u32[]{:S(2)}, u32[]{:S(2)}) collective-permute-start(bf16[2,128,128]{2,1,0:T(8,128)(2,1)S(1)} %shard_map.113), channel_id=1, source_target_pairs={{8,0},{16,8},{24,16},{9,1},{17,9},{25,17},{10,2},{18,10},{26,18},{... | collective-permute-start | bytes 196616 | tf_op jit(solution)/shard_map/ppermute | solution.py:409
  85.9 26.1 %collective-permute-start.3 = (bf16[2,128,128]{2,1,0:T(8,128)(2,1)S(1)}, bf16[2,128,128]{2,1,0:T(8,128)(2,1)S(1)}, u32[]{:S(2)}, u32[]{:S(2)}) collective-permute-start(bf16[2,128,128]{2,1,0:T(8,128)(2,1)S(1)} %shard_map.113), channel_id=1, source_target_pairs={{16,0},{24,8},{17,1},{25,9},{18,2},{26,10},{19,3},{27,11},{20,4},{... | collective-permute-start | bytes 196616 | tf_op jit(solution)/shard_map/ppermute | solution.py:409
  87.2 28.1 %collective-permute-start.4 = (bf16[2,128,128]{2,1,0:T(8,128)(2,1)S(1)}, bf16[2,128,128]{2,1,0:T(8,128)(2,1)S(1)}, u32[]{:S(2)}, u32[]{:S(2)}) collective-permute-start(bf16[2,128,128]{2,1,0:T(8,128)(2,1)S(1)} %shard_map.113), channel_id=1, source_target_pairs={{24,0},{25,1},{26,2},{27,3},{28,4},{29,5},{30,6},{31,7}} | collective-permute-start | bytes 196616 | tf_op jit(solution)/shard_map/ppermute | solution.py:409
  96.5 44.5 %collective-permute-start.6 = (bf16[160,2048]{1,0:T(8,128)(2,1)S(1)}, bf16[160,2048]{1,0:T(8,128)(2,1)S(1)}, u32[]{:S(2)}, u32[]{:S(2)}) collective-permute-start(bf16[160,2048]{1,0:T(8,128)(2,1)S(1)} %get-tuple-element.44), channel_id=1, source_target_pairs={{0,8},{8,0},{16,24},{24,16},{1,9},{9,1},{17,25},{25,17},{2,10},{10... | collective-permute-start | bytes 1966088 | tf_op jit(solution)/shard_map/ppermute | solution.py:335
  110.6 4.7 %copy-start.1 = (bf16[8,144,256]{2,1,0:T(8,128)(2,1)S(1)}, bf16[8,144,256]{2,1,0:T(8,128)(2,1)}, u32[]{:S(2)}) copy-start(bf16[8,144,256]{2,1,0:T(8,128)(2,1)} %all_to_all.36.key_ref) | copy-start | bytes 1769476
  110.8 30.2 %collective-permute-start.8 = (bf16[160,2048]{1,0:T(8,128)(2,1)S(1)}, bf16[160,2048]{1,0:T(8,128)(2,1)S(1)}, u32[]{:S(2)}, u32[]{:S(2)}) collective-permute-start(bf16[160,2048]{1,0:T(8,128)(2,1)S(1)} %add_convert_fusion), channel_id=1, source_target_pairs={{0,16},{8,24},{16,0},{24,8},{1,17},{9,25},{17,1},{25,9},{2,18},{10... | collective-permute-start | bytes 1966088 | tf_op jit(solution)/shard_map/ppermute | solution.py:335
  118.0 23.0 %copy-start = (bf16[1,1024,512]{2,1,0:T(8,128)(2,1)S(1)}, bf16[1,1024,512]{2,1,0:T(8,128)(2,1)}, u32[]{:S(2)}) copy-start(bf16[1,1024,512]{2,1,0:T(8,128)(2,1)} %param.14) | copy-start | bytes 3145732
  142.8 3.5 %copy-start.8 = (bf16[160,2048]{1,0:T(8,128)(2,1)}, bf16[160,2048]{1,0:T(8,128)(2,1)S(1)}, u32[]{:S(2)}) copy-start(bf16[160,2048]{1,0:T(8,128)(2,1)S(1)} %get-tuple-element.53.rest_0_) | copy-start | bytes 1966084
  142.8 32.5 %collective-permute-start.10 = (bf16[160,2048]{1,0:T(8,128)(2,1)S(1)}, bf16[160,2048]{1,0:T(8,128)(2,1)}, u32[]{:S(2)}, u32[]{:S(2)}) collective-permute-start(bf16[160,2048]{1,0:T(8,128)(2,1)S(1)} %get-tuple-element.53.rest_0_), channel_id=1, source_target_pairs={{0,16},{8,24},{16,0},{24,8},{1,17},{9,25},{17,1},{25,9},{2,18},{10... | collective-permute-start | bytes 1966088 | tf_op jit(solution)/shard_map/ppermute | solution.py:335
  142.9 32.4 %collective-permute-start.9 = (bf16[160,2048]{1,0:T(8,128)(2,1)S(1)}, bf16[160,2048]{1,0:T(8,128)(2,1)S(1)}, u32[]{:S(2)}, u32[]{:S(2)}) collective-permute-start(bf16[160,2048]{1,0:T(8,128)(2,1)S(1)} %get-tuple-element.53.rest_0_), channel_id=1, source_target_pairs={{0,8},{8,0},{16,24},{24,16},{1,9},{9,1},{17,25},{25,17},{2,10},{10... | collective-permute-start | bytes 1966088 | tf_op jit(solution)/shard_map/ppermute | solution.py:335
  165.1 8.2 %collective-permute-start.11 = (bf16[2,128,128]{2,1,0:T(8,128)(2,1)S(1)}, bf16[2,128,128]{2,1,0:T(8,128)(2,1)S(1)}, u32[]{:S(2)}, u32[]{:S(2)}) collective-permute-start(bf16[2,128,128]{2,1,0:T(8,128)(2,1)S(1)} %get-tuple-element.52), channel_id=1, source_target_pairs={{0,8},{8,16},{16,24},{1,9},{9,17},{17,25},{2,10},{10,18},{18,26},{... | collective-permute-start | bytes 196616 | tf_op jit(solution)/shard_map/ppermute | solution.py:464
  167.0 7.5 %collective-permute-start.12 = (bf16[2,128,128]{2,1,0:T(8,128)(2,1)S(1)}, bf16[2,128,128]{2,1,0:T(8,128)(2,1)S(1)}, u32[]{:S(2)}, u32[]{:S(2)}) collective-permute-start(bf16[2,128,128]{2,1,0:T(8,128)(2,1)S(1)} %get-tuple-element.52), channel_id=1, source_target_pairs={{0,16},{8,24},{1,17},{9,25},{2,18},{10,26},{3,19},{11,27},{4,20},{... | collective-permute-start | bytes 196616 | tf_op jit(solution)/shard_map/ppermute | solution.py:464
  171.8 3.5 %collective-permute-start.13 = (bf16[2,128,128]{2,1,0:T(8,128)(2,1)S(1)}, bf16[2,128,128]{2,1,0:T(8,128)(2,1)S(1)}, u32[]{:S(2)}, u32[]{:S(2)}) collective-permute-start(bf16[2,128,128]{2,1,0:T(8,128)(2,1)S(1)} %get-tuple-element.52), channel_id=1, source_target_pairs={{0,24},{1,25},{2,26},{3,27},{4,28},{5,29},{6,30},{7,31}} | collective-permute-start | bytes 196616 | tf_op jit(solution)/shard_map/ppermute | solution.py:464
  175.3 4.2 %copy-start.10 = (bf16[160,2048]{1,0:T(8,128)(2,1)}, bf16[160,2048]{1,0:T(8,128)(2,1)S(1)}, u32[]{:S(2)}) copy-start(bf16[160,2048]{1,0:T(8,128)(2,1)S(1)} %collective-permute-done.9.rest_1_) | copy-start | bytes 1966084
  175.3 18.1 %collective-permute-start.14 = (bf16[160,2048]{1,0:T(8,128)(2,1)}, bf16[160,2048]{1,0:T(8,128)(2,1)}, u32[]{:S(2)}, u32[]{:S(2)}) collective-permute-start(bf16[160,2048]{1,0:T(8,128)(2,1)} %collective-permute-done.10.rest_2_), channel_id=1, source_target_pairs={{0,8},{8,0},{16,24},{24,16},{1,9},{9,1},{17,25},{25,17},{2,10},{10... | collective-permute-start | bytes 1966088 | tf_op jit(solution)/shard_map/ppermute | solution.py:335
  179.5 13.9 %copy-start.5 = (bf16[1,512,1024]{2,1,0:T(8,128)(2,1)S(1)}, bf16[1,512,1024]{2,1,0:T(8,128)(2,1)}, u32[]{:S(2)}) copy-start(bf16[1,512,1024]{2,1,0:T(8,128)(2,1)} %param.12) | copy-start | bytes 3145732
  179.5 13.9 %copy-start.7 = (bf16[1,512,1024]{2,1,0:T(8,128)(2,1)S(1)}, bf16[1,512,1024]{2,1,0:T(8,128)(2,1)}, u32[]{:S(2)}) copy-start(bf16[1,512,1024]{2,1,0:T(8,128)(2,1)} %param.13) | copy-start | bytes 3145732
  179.5 20.1 %all-to-all-start.6 = ((bf16[8,256,256]{2,1,0:T(8,128)(2,1)}), bf16[8,256,256]{2,1,0:T(8,128)(2,1)S(1)}, u32[]{:S(2)}, u32[]{:S(2)}) async-start(bf16[8,256,256]{2,1,0:T(8,128)(2,1)} %bitcast.5), calls=%async_computation.6 | async-start | bytes 2097152 | tf_op jit(solution)/shard_map/all_to_all | solution.py:326
  193.4 1.1 copy-start.9
  194.5 1.1 copy-start.11
  199.6 27.4 %all-to-all-start.5 = ((bf16[32,20,512]{2,1,0:T(8,128)(2,1)}), bf16[32,20,512]{2,1,0:T(8,128)(2,1)S(1)}, u32[]{:S(2)}, u32[]{:S(2)}) async-start(bf16[32,20,512]{2,1,0:T(8,128)(2,1)} %shard_map.119), calls=%async_computation.5 | async-start | bytes 1572864 | tf_op jit(solution)/shard_map/all_to_all | solution.py:326
  (1 other events, 1.0 us)

commit v4 on v3

--- a/solution.py
+++ b/solution.py
@@ -176,17 +176,20 @@
             out_ref[place] = product[:, b * part : (b + 1) * part]
 
 
-def backward_kernel(ctx, exp, capacity, pad, me_ref, gate_ref, up_ref, *rest):
-    chunks, (out_ref, grads) = rest[:-2], rest[-2:]
+def backward_kernel(exp, capacity, pad, offsets, me_ref, gate_ref, up_ref, *rest):
+    count = len(offsets)
+    chunks, before, (out_ref, grads) = rest[:count], rest[count:-2], rest[-2:]
     hidden = gate_ref.shape[1]
     slots = exp * capacity
-    for offset in range(ctx):
-        grads[offset * slots : (offset + 1) * slots, :] = chunks[offset][...]
+    for ref in before:
+        out_ref[...] = ref[...]
+    for n in range(count):
+        grads[n * slots : (n + 1) * slots, :] = chunks[n][...]
     product = (dot_nt(grads[:, :hidden], gate_ref[...]) + dot_nt(grads[:, hidden:], up_ref[...])).astype(BF16)
     spread = unpacking(exp, capacity, pad)
-    for offset in range(ctx):
+    for n, offset in enumerate(offsets):
         chunk = me_ref[0] ^ offset
-        rows = dot(spread, product[offset * slots : (offset + 1) * slots]).astype(BF16)
+        rows = dot(spread, product[n * slots : (n + 1) * slots]).astype(BF16)
         for e in range(exp):
             out_ref[chunk * exp + e] = rows[e * pad : e * pad + capacity]
 
@@ -466,13 +469,16 @@
     chunks, state_in = lax.optimization_barrier((chunks, state_in))
     chunks = spread_rest(chunks, doubling)
     chunks = [chunks[o] for o in range(ctx)]
-    (outgoing,) = run(
-        functools.partial(backward_kernel, ctx, exp, capacity, pad),
-        [shape((ctx * exp, capacity, slice_width), BF16)],
-        [me, weight_gate[0], weight_up[0], *chunks],
-        scratch=[pltpu.VMEM((ctx * slots, 2 * hidden), BF16)],
-        us=60,
-    )
+    before = []
+    for offsets in (tuple(range(ctx - 1)), (ctx - 1,)):
+        before = run(
+            functools.partial(backward_kernel, exp, capacity, pad, offsets),
+            [shape((ctx * exp, capacity, slice_width), BF16)],
+            [me, weight_gate[0], weight_up[0], *(chunks[o] for o in offsets), *before],
+            scratch=[pltpu.VMEM((len(offsets) * slots, 2 * hidden), BF16)],
+            us=60 if len(offsets) == 1 else 3,
+        )
+    (outgoing,) = before
     (heads_back,) = run(
         functools.partial(finish_kernel, heads, scale),
         [shape((2 * exp, rows, key_width), BF16)],

time: 229 us -> 227 us (level)
  waiting for transfers between devices: 96.7 us -> 94.2 us
    ppermute x9, waiting for transfers between devices: 52.9 us -> 48.1 us  [swap(): return lax.ppermute(block, CTX, [(i, i ^ distance) for i in range(count)])]
    pallas_call x11 -> x12, Pallas kernels: 22.4 us -> 24 us  [run(): pl.pallas_call(kernel, out_shape=tuple(outs), in_specs=in_specs, out_spec...]
  transfers between devices with their start and end apart: 18 -> 18, of which waited for: 12 -> 13; matrix products, arithmetic and copies ran while one was open for 1% -> 1% of each run, Pallas kernels for 8% -> 9%
where the time goes in v4:
time: 227 us; the launch traced here: 225 us
  waiting for transfers between devices  94.2 us (41%)
  blocking collectives  56.3 us (25%)
  starting transfers between devices  40.7 us (18%)
  Pallas kernels  24 us (11%)
  local copies, waits for them, and re-layouts  9.29 us (4%)
    all_to_all x4, blocking collectives, move(): return lax.all_to_all(buffer, axes, split_axis=0, concat_axis=0, tiled=True)  56.3 us
    ppermute x9, waiting for transfers between devices, swap(): return lax.ppermute(block, CTX, [(i, i ^ distance) for i in range(count)])  48.1 us
    all_to_all x3, waiting for transfers between devices, move(): return lax.all_to_all(buffer, axes, split_axis=0, concat_axis=0, tiled=True)  40.7 us
    pallas_call x12, Pallas kernels, run(): pl.pallas_call(kernel, out_shape=tuple(outs), in_specs=in_specs, out_spec...  24 us
    ppermute x9, starting transfers between devices, swap(): return lax.ppermute(block, CTX, [(i, i ^ distance) for i in range(count)])  15.4 us
    all_to_all x3, starting transfers between devices, move(): return lax.all_to_all(buffer, axes, split_axis=0, concat_axis=0, tiled=True)  13.3 us
    unnamed x32, local copies, waits for them, and re-layouts  9.29 us
    ppermute x3, starting transfers between devices, shards(): lax.ppermute(state, CTX, [(i, i + step) for i in range(ctx - step)])  8.15 us
  transfers between devices with their start and end apart: 18, of which 13 were waited for; matrix products, arithmetic and copies ran while one was open for 1% of the time, Pallas kernels for 9%

profile of v4, /device:TPU:0, one launch (start us, length us, event | category | flops | bytes accessed | tf_op | source)
XLA Modules:
  0.0 225.5 jit_solution(11604970756773355953)
XLA Ops:
  0.6 3.1 %collective-permute-start = (bf16[1024,512]{1,0:T(8,128)(2,1)}, bf16[1024,512]{1,0:T(8,128)(2,1)S(1)}, u32[]{:S(2)}, u32[]{:S(2)}) collective-permute-start(bf16[1024,512]{1,0:T(8,128)(2,1)} %bitcast.6), channel_id=1, source_target_pairs={{0,8},{8,0},{16,24},{24,16},{1,9},{9,1},{17,25},{25,17},{2,10},{10... | collective-permute-start | bytes 3145736 | tf_op jit(solution)/shard_map/ppermute | solution.py:338
  3.7 2.6 %collective-permute-start.1 = (bf16[1024,512]{1,0:T(8,128)(2,1)}, bf16[1024,512]{1,0:T(8,128)(2,1)S(1)}, u32[]{:S(2)}, u32[]{:S(2)}) collective-permute-start(bf16[1024,512]{1,0:T(8,128)(2,1)} %bitcast.7), channel_id=1, source_target_pairs={{0,16},{8,24},{16,0},{24,8},{1,17},{9,25},{17,1},{25,9},{2,18},{10... | collective-permute-start | bytes 3145736 | tf_op jit(solution)/shard_map/ppermute | solution.py:338
  11.0 1.7 shard_map.112
  12.7 13.4 %all_to_all.35 = bf16[8,128,256]{2,1,0:T(8,128)(2,1)} all-to-all(bf16[8,128,256]{2,1,0:T(8,128)(2,1)S(1)} %get-tuple-element.34), channel_id=1, replica_groups=mesh['hi'=2,'lo'=2,'exp'=8] {'exp'}, dimensions={0} | all-to-all | bytes 1048576 | tf_op jit(solution)/shard_map/all_to_all | solution.py:329
  26.0 13.5 %all_to_all.36.key_ref = bf16[8,144,256]{2,1,0:T(8,128)(2,1)} all-to-all(bf16[8,144,256]{2,1,0:T(8,128)(2,1)S(1)} %get-tuple-element.37), channel_id=1, replica_groups=mesh['hi'=2,'lo'=2,'exp'=8] {'exp'}, dimensions={0} | all-to-all | bytes 1179648 | tf_op jit(solution)/shard_map/all_to_all | solution.py:329
  39.5 9.9 %collective-permute-done.rest_4_.rest_1_ = bf16[1024,512]{1,0:T(8,128)(2,1)S(1)} collective-permute-done((bf16[1024,512]{1,0:T(8,128)(2,1)}, bf16[1024,512]{1,0:T(8,128)(2,1)S(1)}, u32[]{:S(2)}, u32[]{:S(2)}) %collective-permute-start) | collective-permute-done | bytes 1048608 | tf_op jit(solution)/shard_map/ppermute | solution.py:338
  49.4 2.5 %collective-permute-done.1.rest_5_.rest_2_ = bf16[1024,512]{1,0:T(8,128)(2,1)S(1)} collective-permute-done((bf16[1024,512]{1,0:T(8,128)(2,1)}, bf16[1024,512]{1,0:T(8,128)(2,1)S(1)}, u32[]{:S(2)}, u32[]{:S(2)}) %collective-permute-start.1) | collective-permute-done | bytes 1048608 | tf_op jit(solution)/shard_map/ppermute | solution.py:338
  52.0 4.8 %all-to-all-start.3 = ((bf16[32,20,512]{2,1,0:T(8,128)(2,1)}), bf16[32,20,512]{2,1,0:T(8,128)(2,1)}, u32[]{:S(2)}, u32[]{:S(2)}) async-start(bf16[32,20,512]{2,1,0:T(8,128)(2,1)} %get-tuple-element.40), calls=%async_computation.3 | async-start | bytes 1572864 | tf_op jit(solution)/shard_map/all_to_all | solution.py:329
  56.8 1.8 collective-permute-start.5
  58.6 18.9 %all-to-all-done.3.in_ref = bf16[32,20,512]{2,1,0:T(8,128)(2,1)} async-done(((bf16[32,20,512]{2,1,0:T(8,128)(2,1)}), bf16[32,20,512]{2,1,0:T(8,128)(2,1)}, u32[]{:S(2)}, u32[]{:S(2)}) %all-to-all-start.3) | async-done | bytes 655392 | tf_op jit(solution)/shard_map/all_to_all | solution.py:329
  79.9 2.9 %shard_map.115 = (f32[160,2048]{1,0:T(8,128)S(1)}, bf16[160,2048]{1,0:T(8,128)(2,1)S(1)}, f32[160,2048]{1,0:T(8,128)S(1)}, bf16[160,2048]{1,0:T(8,128)(2,1)S(1)}) custom-call(s32[1]{0:T(128)} %bitcast.me_ref, bf16[32,20,512]{2,1,0:T(8,128)(2,1)} %all-to-all-done.3.in_ref, bf16[512,1024]{1,0:T(8,128)(2,1)S(1)} %bitcast.13, bf16[512,1024]{1,0:T(8,128)(2,1)S(1)} %bitcast.16), custom_call_target="tpu_custom_call" | custom-call | flops 4600000000 | bytes 66846 | tf_op jit(solution)/shard_map/pallas_call | solution.py:42
  88.5 8.0 %collective-permute-done.5.rest_6_.rest_3_ = bf16[1024,512]{1,0:T(8,128)(2,1)S(1)} collective-permute-done((bf16[1024,512]{1,0:T(8,128)(2,1)S(1)}, bf16[1024,512]{1,0:T(8,128)(2,1)S(1)}, u32[]{:S(2)}, u32[]{:S(2)}) %collective-permute-start.5) | collective-permute-done | bytes 1048608 | tf_op jit(solution)/shard_map/ppermute | solution.py:338
  96.5 14.0 %collective-permute-done.7 = bf16[160,2048]{1,0:T(8,128)(2,1)S(1)} collective-permute-done((bf16[160,2048]{1,0:T(8,128)(2,1)S(1)}, bf16[160,2048]{1,0:T(8,128)(2,1)S(1)}, u32[]{:S(2)}, u32[]{:S(2)}) %collective-permute-start.7) | collective-permute-done | bytes 655392 | tf_op jit(solution)/shard_map/ppermute | solution.py:338
  112.0 3.3 %collective-permute-done.4.rest_2_ = bf16[2,128,128]{2,1,0:T(8,128)(2,1)S(1)} collective-permute-done((bf16[2,128,128]{2,1,0:T(8,128)(2,1)S(1)}, bf16[2,128,128]{2,1,0:T(8,128)(2,1)S(1)}, u32[]{:S(2)}, u32[]{:S(2)}) %collective-permute-start.4) | collective-permute-done | bytes 65568 | tf_op jit(solution)/shard_map/ppermute | solution.py:412
  115.3 2.7 %shard_map.114 = (bf16[8,160,256]{2,1,0:T(8,128)(2,1)S(1)}, bf16[4,128,128]{2,1,0:T(8,128)(2,1)S(1)}) custom-call(bf16[1024,256]{1,0:T(8,128)(2,1)S(1)} %bitcast.11, bf16[8,144,256]{2,1,0:T(8,128)(2,1)S(1)} %copy-done.1, bf16[1024,256]{1,0:T(8,128)(2,1)S(1)} %copy-done.2, bf16[2,128,128]{2,1,0:T(8,128)(2,1)S(1)} %collective-permute-done.2.rest_0_, ...), custom_call_target="tpu_custom_call" | custom-call | flops 3449999872 | bytes 26214 | tf_op jit(solution)/shard_map/pallas_call | solution.py:42
  118.0 14.8 %all_to_all.37.grads_ref = bf16[8,160,256]{2,1,0:T(8,128)(2,1)S(1)} all-to-all(bf16[8,160,256]{2,1,0:T(8,128)(2,1)S(1)} %get-tuple-element.39), channel_id=1, replica_groups=mesh['hi'=2,'lo'=2,'exp'=8] {'exp'}, dimensions={0} | all-to-all | bytes 1310720 | tf_op jit(solution)/shard_map/all_to_all | solution.py:329
  132.8 8.3 %collective-permute-done.6.rest_1_ = bf16[160,2048]{1,0:T(8,128)(2,1)S(1)} collective-permute-done((bf16[160,2048]{1,0:T(8,128)(2,1)S(1)}, bf16[160,2048]{1,0:T(8,128)(2,1)S(1)}, u32[]{:S(2)}, u32[]{:S(2)}) %collective-permute-start.6) | collective-permute-done | bytes 655392 | tf_op jit(solution)/shard_map/ppermute | solution.py:338
  141.0 1.7 shard_map.116
  142.9 2.5 %collective-permute-start.9 = (bf16[160,2048]{1,0:T(8,128)(2,1)S(1)}, bf16[160,2048]{1,0:T(8,128)(2,1)S(1)}, u32[]{:S(2)}, u32[]{:S(2)}) collective-permute-start(bf16[160,2048]{1,0:T(8,128)(2,1)S(1)} %get-tuple-element.54.rest_0_), channel_id=1, source_target_pairs={{0,8},{8,0},{16,24},{24,16},{1,9},{9,1},{17,25},{25,17},{2,10},{10... | collective-permute-start | bytes 1966088 | tf_op jit(solution)/shard_map/ppermute | solution.py:338
  146.3 14.6 %all_to_all.38.in_ref = bf16[8,160,256]{2,1,0:T(8,128)(2,1)S(1)} all-to-all(bf16[8,160,256]{2,1,0:T(8,128)(2,1)S(1)} %shard_map.117), channel_id=1, replica_groups=mesh['hi'=2,'lo'=2,'exp'=8] {'exp'}, dimensions={0} | all-to-all | bytes 1310720 | tf_op jit(solution)/shard_map/all_to_all | solution.py:329
  160.9 4.2 %shard_map.118 = (bf16[1024,256]{1,0:T(8,128)(2,1)S(1)}, f32[1024,256]{1,0:T(8,128)S(1)}, bf16[2,128,128]{2,1,0:T(8,128)(2,1)S(1)}) custom-call(bf16[1024,256]{1,0:T(8,128)(2,1)S(1)} %bitcast.12, bf16[8,144,256]{2,1,0:T(8,128)(2,1)S(1)} %copy-done.1, bf16[1024,256]{1,0:T(8,128)(2,1)S(1)} %copy-done.2, bf16[4,128,128]{2,1,0:T(8,128)(2,1)S(1)} %get-tuple-element.50.low_ref, ...), custom_call_target="tpu_custom_call" | custom-call | bytes 40632 | tf_op jit(solution)/shard_map/pallas_call | solution.py:42
  165.1 1.9 collective-permute-start.11
  167.0 4.7 %collective-permute-start.12 = (bf16[2,128,128]{2,1,0:T(8,128)(2,1)S(1)}, bf16[2,128,128]{2,1,0:T(8,128)(2,1)S(1)}, u32[]{:S(2)}, u32[]{:S(2)}) collective-permute-start(bf16[2,128,128]{2,1,0:T(8,128)(2,1)S(1)} %get-tuple-element.52), channel_id=1, source_target_pairs={{0,16},{8,24},{1,17},{9,25},{2,18},{10,26},{3,19},{11,27},{4,20},{... | collective-permute-start | bytes 196616 | tf_op jit(solution)/shard_map/ppermute | solution.py:467
  171.8 1.5 collective-permute-start.13
  175.3 2.9 %collective-permute-start.14 = (bf16[160,2048]{1,0:T(8,128)(2,1)}, bf16[160,2048]{1,0:T(8,128)(2,1)}, u32[]{:S(2)}, u32[]{:S(2)}) collective-permute-start(bf16[160,2048]{1,0:T(8,128)(2,1)} %collective-permute-done.10.rest_2_), channel_id=1, source_target_pairs={{0,8},{8,0},{16,24},{24,16},{1,9},{9,1},{17,25},{25,17},{2,10},{10... | collective-permute-start | bytes 1966088 | tf_op jit(solution)/shard_map/ppermute | solution.py:338
  179.5 3.8 %all-to-all-start.6 = ((bf16[8,256,256]{2,1,0:T(8,128)(2,1)}), bf16[8,256,256]{2,1,0:T(8,128)(2,1)S(1)}, u32[]{:S(2)}, u32[]{:S(2)}) async-start(bf16[8,256,256]{2,1,0:T(8,128)(2,1)} %bitcast.5), calls=%async_computation.6 | async-start | bytes 2097152 | tf_op jit(solution)/shard_map/all_to_all | solution.py:329
  185.5 2.6 %shard_map.119.rest_1_ = bf16[32,20,512]{2,1,0:T(8,128)(2,1)S(1)} custom-call(s32[1]{0:T(128)} %bitcast.me_ref, bf16[512,1024]{1,0:T(8,128)(2,1)S(1)} %bitcast.14, bf16[512,1024]{1,0:T(8,128)(2,1)S(1)} %bitcast.17, bf16[160,2048]{1,0:T(8,128)(2,1)S(1)} %copy-done.9, bf16[160,2048]{1,0:T(8,128)(2,1)S(1)} %copy-done.11, ...), custom_call_target="tpu_custom_call" | custom-call | flops 3449999872 | bytes 47185 | tf_op jit(solution)/shard_map/pallas_call | solution.py:42
  188.1 5.4 %collective-permute-done.14.rest_0_ = bf16[160,2048]{1,0:T(8,128)(2,1)} collective-permute-done((bf16[160,2048]{1,0:T(8,128)(2,1)}, bf16[160,2048]{1,0:T(8,128)(2,1)}, u32[]{:S(2)}, u32[]{:S(2)}) %collective-permute-start.14) | collective-permute-done | bytes 655392 | tf_op jit(solution)/shard_map/ppermute | solution.py:338
  193.4 3.0 %shard_map.120 = bf16[32,20,512]{2,1,0:T(8,128)(2,1)} custom-call(s32[1]{0:T(128)} %bitcast.me_ref, bf16[512,1024]{1,0:T(8,128)(2,1)S(1)} %bitcast.15, bf16[512,1024]{1,0:T(8,128)(2,1)S(1)} %bitcast.18, bf16[160,2048]{1,0:T(8,128)(2,1)} %collective-permute-done.14.rest_0_, bf16[32,20,512]{2,1,0:T(8,128)(2,1)S(1)} %shard_map.119.rest_1_), custom_call_target="tpu_custom_call" | custom-call | flops 69000003584 | bytes 40632 | tf_op jit(solution)/shard_map/pallas_call | solution.py:42
  196.5 2.3 %all-to-all-done.6.in_ref = bf16[8,256,256]{2,1,0:T(8,128)(2,1)S(1)} async-done(((bf16[8,256,256]{2,1,0:T(8,128)(2,1)}), bf16[8,256,256]{2,1,0:T(8,128)(2,1)S(1)}, u32[]{:S(2)}, u32[]{:S(2)}) %all-to-all-start.6) | async-done | bytes 1048608 | tf_op jit(solution)/shard_map/all_to_all | solution.py:329
  198.7 4.7 %all-to-all-start.5 = ((bf16[32,20,512]{2,1,0:T(8,128)(2,1)}), bf16[32,20,512]{2,1,0:T(8,128)(2,1)S(1)}, u32[]{:S(2)}, u32[]{:S(2)}) async-start(bf16[32,20,512]{2,1,0:T(8,128)(2,1)} %shard_map.120), calls=%async_computation.5 | async-start | bytes 1572864 | tf_op jit(solution)/shard_map/all_to_all | solution.py:329
  204.5 19.5 %all-to-all-done.5.in_ref = bf16[32,20,512]{2,1,0:T(8,128)(2,1)S(1)} async-done(((bf16[32,20,512]{2,1,0:T(8,128)(2,1)}), bf16[32,20,512]{2,1,0:T(8,128)(2,1)S(1)}, u32[]{:S(2)}, u32[]{:S(2)}) %all-to-all-start.5) | async-done | bytes 655392 | tf_op jit(solution)/shard_map/all_to_all | solution.py:329
  (53 shorter events, 23.1 us)
Async XLA Ops:
  0.6 48.8 %collective-permute-start = (bf16[1024,512]{1,0:T(8,128)(2,1)}, bf16[1024,512]{1,0:T(8,128)(2,1)S(1)}, u32[]{:S(2)}, u32[]{:S(2)}) collective-permute-start(bf16[1024,512]{1,0:T(8,128)(2,1)} %bitcast.6), channel_id=1, source_target_pairs={{0,8},{8,0},{16,24},{24,16},{1,9},{9,1},{17,25},{25,17},{2,10},{10... | collective-permute-start | bytes 3145736 | tf_op jit(solution)/shard_map/ppermute | solution.py:338
  3.7 48.3 %collective-permute-start.1 = (bf16[1024,512]{1,0:T(8,128)(2,1)}, bf16[1024,512]{1,0:T(8,128)(2,1)S(1)}, u32[]{:S(2)}, u32[]{:S(2)}) collective-permute-start(bf16[1024,512]{1,0:T(8,128)(2,1)} %bitcast.7), channel_id=1, source_target_pairs={{0,16},{8,24},{16,0},{24,8},{1,17},{9,25},{17,1},{25,9},{2,18},{10... | collective-permute-start | bytes 3145736 | tf_op jit(solution)/shard_map/ppermute | solution.py:338
  7.8 1.0 copy-start.12
  8.9 1.0 copy-start.13
  52.0 25.5 %all-to-all-start.3 = ((bf16[32,20,512]{2,1,0:T(8,128)(2,1)}), bf16[32,20,512]{2,1,0:T(8,128)(2,1)}, u32[]{:S(2)}, u32[]{:S(2)}) async-start(bf16[32,20,512]{2,1,0:T(8,128)(2,1)} %get-tuple-element.40), calls=%async_computation.3 | async-start | bytes 1572864 | tf_op jit(solution)/shard_map/all_to_all | solution.py:329
  56.8 39.7 %collective-permute-start.5 = (bf16[1024,512]{1,0:T(8,128)(2,1)S(1)}, bf16[1024,512]{1,0:T(8,128)(2,1)S(1)}, u32[]{:S(2)}, u32[]{:S(2)}) collective-permute-start(bf16[1024,512]{1,0:T(8,128)(2,1)S(1)} %collective-permute-done.1.rest_5_.rest_2_), channel_id=1, source_target_pairs={{0,8},{8,0},{16,24},{24,16},{1,9},{9,1},{17,25},{25,17},{2,10},{10... | collective-permute-start | bytes 3145736 | tf_op jit(solution)/shard_map/ppermute | solution.py:338
  77.5 1.2 copy-start.4
  78.7 1.2 copy-start.6
  79.9 4.3 %copy-start.2 = (bf16[1024,256]{1,0:T(8,128)(2,1)S(1)}, bf16[1024,256]{1,0:T(8,128)(2,1)}, u32[]{:S(2)}) copy-start(bf16[1024,256]{1,0:T(8,128)(2,1)} %cot_ref.7) | copy-start | bytes 1572868
  79.9 4.3 %copy-start.3 = (bf16[8,128,256]{2,1,0:T(8,128)(2,1)S(1)}, bf16[8,128,256]{2,1,0:T(8,128)(2,1)}, u32[]{:S(2)}) copy-start(bf16[8,128,256]{2,1,0:T(8,128)(2,1)} %all_to_all.35) | copy-start | bytes 1572868
  82.9 27.7 %collective-permute-start.7 = (bf16[160,2048]{1,0:T(8,128)(2,1)S(1)}, bf16[160,2048]{1,0:T(8,128)(2,1)S(1)}, u32[]{:S(2)}, u32[]{:S(2)}) collective-permute-start(bf16[160,2048]{1,0:T(8,128)(2,1)S(1)} %get-tuple-element.46), channel_id=1, source_target_pairs={{0,8},{8,0},{16,24},{24,16},{1,9},{9,1},{17,25},{25,17},{2,10},{10... | collective-permute-start | bytes 1966088 | tf_op jit(solution)/shard_map/ppermute | solution.py:338
  84.6 27.4 %collective-permute-start.2 = (bf16[2,128,128]{2,1,0:T(8,128)(2,1)S(1)}, bf16[2,128,128]{2,1,0:T(8,128)(2,1)S(1)}, u32[]{:S(2)}, u32[]{:S(2)}) collective-permute-start(bf16[2,128,128]{2,1,0:T(8,128)(2,1)S(1)} %shard_map.113), channel_id=1, source_target_pairs={{8,0},{16,8},{24,16},{9,1},{17,9},{25,17},{10,2},{18,10},{26,18},{... | collective-permute-start | bytes 196616 | tf_op jit(solution)/shard_map/ppermute | solution.py:412
  85.9 26.1 %collective-permute-start.3 = (bf16[2,128,128]{2,1,0:T(8,128)(2,1)S(1)}, bf16[2,128,128]{2,1,0:T(8,128)(2,1)S(1)}, u32[]{:S(2)}, u32[]{:S(2)}) collective-permute-start(bf16[2,128,128]{2,1,0:T(8,128)(2,1)S(1)} %shard_map.113), channel_id=1, source_target_pairs={{16,0},{24,8},{17,1},{25,9},{18,2},{26,10},{19,3},{27,11},{20,4},{... | collective-permute-start | bytes 196616 | tf_op jit(solution)/shard_map/ppermute | solution.py:412
  87.2 28.1 %collective-permute-start.4 = (bf16[2,128,128]{2,1,0:T(8,128)(2,1)S(1)}, bf16[2,128,128]{2,1,0:T(8,128)(2,1)S(1)}, u32[]{:S(2)}, u32[]{:S(2)}) collective-permute-start(bf16[2,128,128]{2,1,0:T(8,128)(2,1)S(1)} %shard_map.113), channel_id=1, source_target_pairs={{24,0},{25,1},{26,2},{27,3},{28,4},{29,5},{30,6},{31,7}} | collective-permute-start | bytes 196616 | tf_op jit(solution)/shard_map/ppermute | solution.py:412
  96.5 44.5 %collective-permute-start.6 = (bf16[160,2048]{1,0:T(8,128)(2,1)S(1)}, bf16[160,2048]{1,0:T(8,128)(2,1)S(1)}, u32[]{:S(2)}, u32[]{:S(2)}) collective-permute-start(bf16[160,2048]{1,0:T(8,128)(2,1)S(1)} %get-tuple-element.44), channel_id=1, source_target_pairs={{0,8},{8,0},{16,24},{24,16},{1,9},{9,1},{17,25},{25,17},{2,10},{10... | collective-permute-start | bytes 1966088 | tf_op jit(solution)/shard_map/ppermute | solution.py:338
  110.6 4.7 %copy-start.1 = (bf16[8,144,256]{2,1,0:T(8,128)(2,1)S(1)}, bf16[8,144,256]{2,1,0:T(8,128)(2,1)}, u32[]{:S(2)}) copy-start(bf16[8,144,256]{2,1,0:T(8,128)(2,1)} %all_to_all.36.key_ref) | copy-start | bytes 1769476
  110.8 30.2 %collective-permute-start.8 = (bf16[160,2048]{1,0:T(8,128)(2,1)S(1)}, bf16[160,2048]{1,0:T(8,128)(2,1)S(1)}, u32[]{:S(2)}, u32[]{:S(2)}) collective-permute-start(bf16[160,2048]{1,0:T(8,128)(2,1)S(1)} %add_convert_fusion), channel_id=1, source_target_pairs={{0,16},{8,24},{16,0},{24,8},{1,17},{9,25},{17,1},{25,9},{2,18},{10... | collective-permute-start | bytes 1966088 | tf_op jit(solution)/shard_map/ppermute | solution.py:338
  118.0 23.0 %copy-start = (bf16[1,1024,512]{2,1,0:T(8,128)(2,1)S(1)}, bf16[1,1024,512]{2,1,0:T(8,128)(2,1)}, u32[]{:S(2)}) copy-start(bf16[1,1024,512]{2,1,0:T(8,128)(2,1)} %param.14) | copy-start | bytes 3145732
  142.8 3.5 %copy-start.8 = (bf16[160,2048]{1,0:T(8,128)(2,1)}, bf16[160,2048]{1,0:T(8,128)(2,1)S(1)}, u32[]{:S(2)}) copy-start(bf16[160,2048]{1,0:T(8,128)(2,1)S(1)} %get-tuple-element.54.rest_0_) | copy-start | bytes 1966084
  142.8 32.5 %collective-permute-start.10 = (bf16[160,2048]{1,0:T(8,128)(2,1)S(1)}, bf16[160,2048]{1,0:T(8,128)(2,1)}, u32[]{:S(2)}, u32[]{:S(2)}) collective-permute-start(bf16[160,2048]{1,0:T(8,128)(2,1)S(1)} %get-tuple-element.54.rest_0_), channel_id=1, source_target_pairs={{0,16},{8,24},{16,0},{24,8},{1,17},{9,25},{17,1},{25,9},{2,18},{10... | collective-permute-start | bytes 1966088 | tf_op jit(solution)/shard_map/ppermute | solution.py:338
  142.9 32.4 %collective-permute-start.9 = (bf16[160,2048]{1,0:T(8,128)(2,1)S(1)}, bf16[160,2048]{1,0:T(8,128)(2,1)S(1)}, u32[]{:S(2)}, u32[]{:S(2)}) collective-permute-start(bf16[160,2048]{1,0:T(8,128)(2,1)S(1)} %get-tuple-element.54.rest_0_), channel_id=1, source_target_pairs={{0,8},{8,0},{16,24},{24,16},{1,9},{9,1},{17,25},{25,17},{2,10},{10... | collective-permute-start | bytes 1966088 | tf_op jit(solution)/shard_map/ppermute | solution.py:338
  165.1 8.2 %collective-permute-start.11 = (bf16[2,128,128]{2,1,0:T(8,128)(2,1)S(1)}, bf16[2,128,128]{2,1,0:T(8,128)(2,1)S(1)}, u32[]{:S(2)}, u32[]{:S(2)}) collective-permute-start(bf16[2,128,128]{2,1,0:T(8,128)(2,1)S(1)} %get-tuple-element.52), channel_id=1, source_target_pairs={{0,8},{8,16},{16,24},{1,9},{9,17},{17,25},{2,10},{10,18},{18,26},{... | collective-permute-start | bytes 196616 | tf_op jit(solution)/shard_map/ppermute | solution.py:467
  167.0 7.5 %collective-permute-start.12 = (bf16[2,128,128]{2,1,0:T(8,128)(2,1)S(1)}, bf16[2,128,128]{2,1,0:T(8,128)(2,1)S(1)}, u32[]{:S(2)}, u32[]{:S(2)}) collective-permute-start(bf16[2,128,128]{2,1,0:T(8,128)(2,1)S(1)} %get-tuple-element.52), channel_id=1, source_target_pairs={{0,16},{8,24},{1,17},{9,25},{2,18},{10,26},{3,19},{11,27},{4,20},{... | collective-permute-start | bytes 196616 | tf_op jit(solution)/shard_map/ppermute | solution.py:467
  171.8 3.5 %collective-permute-start.13 = (bf16[2,128,128]{2,1,0:T(8,128)(2,1)S(1)}, bf16[2,128,128]{2,1,0:T(8,128)(2,1)S(1)}, u32[]{:S(2)}, u32[]{:S(2)}) collective-permute-start(bf16[2,128,128]{2,1,0:T(8,128)(2,1)S(1)} %get-tuple-element.52), channel_id=1, source_target_pairs={{0,24},{1,25},{2,26},{3,27},{4,28},{5,29},{6,30},{7,31}} | collective-permute-start | bytes 196616 | tf_op jit(solution)/shard_map/ppermute | solution.py:467
  175.3 4.2 %copy-start.10 = (bf16[160,2048]{1,0:T(8,128)(2,1)}, bf16[160,2048]{1,0:T(8,128)(2,1)S(1)}, u32[]{:S(2)}) copy-start(bf16[160,2048]{1,0:T(8,128)(2,1)S(1)} %collective-permute-done.9.rest_1_) | copy-start | bytes 1966084
  175.3 18.1 %collective-permute-start.14 = (bf16[160,2048]{1,0:T(8,128)(2,1)}, bf16[160,2048]{1,0:T(8,128)(2,1)}, u32[]{:S(2)}, u32[]{:S(2)}) collective-permute-start(bf16[160,2048]{1,0:T(8,128)(2,1)} %collective-permute-done.10.rest_2_), channel_id=1, source_target_pairs={{0,8},{8,0},{16,24},{24,16},{1,9},{9,1},{17,25},{25,17},{2,10},{10... | collective-permute-start | bytes 1966088 | tf_op jit(solution)/shard_map/ppermute | solution.py:338
  179.5 3.8 %copy-start.5 = (bf16[1,512,1024]{2,1,0:T(8,128)(2,1)S(1)}, bf16[1,512,1024]{2,1,0:T(8,128)(2,1)}, u32[]{:S(2)}) copy-start(bf16[1,512,1024]{2,1,0:T(8,128)(2,1)} %param.12) | copy-start | bytes 3145732
  179.5 3.8 %copy-start.7 = (bf16[1,512,1024]{2,1,0:T(8,128)(2,1)S(1)}, bf16[1,512,1024]{2,1,0:T(8,128)(2,1)}, u32[]{:S(2)}) copy-start(bf16[1,512,1024]{2,1,0:T(8,128)(2,1)} %param.13) | copy-start | bytes 3145732
  179.5 19.2 %all-to-all-start.6 = ((bf16[8,256,256]{2,1,0:T(8,128)(2,1)}), bf16[8,256,256]{2,1,0:T(8,128)(2,1)S(1)}, u32[]{:S(2)}, u32[]{:S(2)}) async-start(bf16[8,256,256]{2,1,0:T(8,128)(2,1)} %bitcast.5), calls=%async_computation.6 | async-start | bytes 2097152 | tf_op jit(solution)/shard_map/all_to_all | solution.py:329
  183.3 1.1 copy-start.9
  184.4 1.1 copy-start.11
  198.7 25.3 %all-to-all-start.5 = ((bf16[32,20,512]{2,1,0:T(8,128)(2,1)}), bf16[32,20,512]{2,1,0:T(8,128)(2,1)S(1)}, u32[]{:S(2)}, u32[]{:S(2)}) async-start(bf16[32,20,512]{2,1,0:T(8,128)(2,1)} %shard_map.120), calls=%async_computation.5 | async-start | bytes 1572864 | tf_op jit(solution)/shard_map/all_to_all | solution.py:329
  (1 other events, 1.0 us)
